TPU v7x, 128 devices: a whole 4x4x4 slice. The times are simulated.
128 devices in a mesh: ctx: 16 (over y_hi, x, core), grp: 8 (over z, y_lo).
Axes of the slice: x: 4, y: 4 (y_hi: 2, y_lo: 2; y = y_hi * 2 + y_lo), z: 4, core: 2. Of those that a mesh axis runs over, the one named last changes fastest.
Arguments:
- queries: bfloat16 [8, 8192, 32, 128], P('grp', 'ctx'), may hold values from -6 to 6
- keys: bfloat16 [8, 8192, 32, 128], P('grp', 'ctx'), may hold values from -0.0625 to 0.0625
- values: bfloat16 [8, 8192, 32, 128], P('grp', 'ctx'), may hold values from -6 to 6
- prefill_decay: float32 [8, 8192, 32], P('grp', 'ctx'), may hold values from -0.8 to 0, as said below
- start_states: float32 [8, 32, 128, 128], P('grp', 'ctx'), may hold values from -3 to 3
- resident_states: float32 [64, 32, 128, 128], P(None, 'ctx', None, 'grp'), may hold values from -3 to 3
- slot_of_prompt: int32 [8], replicated, may hold values from 0 to 63, as said below
- decode_queries: bfloat16 [64, 4, 32, 128], P(None, None, 'ctx'), may hold values from -6 to 6
- decode_keys: bfloat16 [64, 4, 32, 128], P(None, None, 'ctx'), may hold values from -1.75 to 1.75
- decode_values: bfloat16 [64, 4, 32, 128], P(None, None, 'ctx', 'grp'), may hold values from -6 to 6
- decode_gate: bfloat16 [64, 4, 32, 128], P(None, None, 'ctx', 'grp'), may hold values from -8 to 8
- decode_decay: float32 [64, 4, 32], P(None, None, 'ctx'), may hold values from -0.8 to 0, as said below
- norm_gain: float32 [32, 128], P('ctx', 'grp'), may hold values from 0.5 to 1.5
- out_weight: bfloat16 [32, 128, 6144], P('ctx', 'grp'), may hold values from -0.09375 to 0.09375
Outputs:
- prefill_out: bfloat16 [8, 8192, 32, 128], P('grp', 'ctx')
- decode_states: float32 [64, 32, 128, 128], P(None, 'ctx', None, 'grp')
- decoded: float32 [256, 6144], P(('ctx', 'grp'))
Inputs may be any that keep to these rules, and one draw needn't show every extreme that they name: `slot_of_prompt`: distinct decode rows; rows 0 and 63 are always among them. `prefill_decay`: strictly negative. `decode_decay`: strictly negative.
All inputs are finite; a program needn't handle non-finite values.
Results may differ from a plain program's by a relative error of at most 0.0029.
Values sent between devices are 32-bit elements; how exact they have to be, the bound alone decides.
A program may use at most 192 MiB of HBM per device.

v0:
```python
import jax
import jax.numpy as jnp
from jax import lax
from jax.sharding import PartitionSpec as P

H = 32
HS = 128


def prefix(array, axis, combine, identity):
    count, mine = (lax.axis_size(axis), lax.axis_index(axis))
    everything = jax.tree.map(lambda part: lax.all_gather(part, axis), array)
    start = jax.tree.map(
        lambda part, zero: jnp.broadcast_to(jnp.asarray(zero, part.dtype), part.shape),
        array,
        identity,
    )

    def step(k, before):
        reached = k < mine
        new = combine(before, jax.tree.map(lambda part: part[k], everything))
        return jax.tree.map(lambda a, b: jnp.where(reached, a, b), new, before)

    return lax.fori_loop(0, count, step, start)


def normalize(field):
    mean_sq = jnp.mean(field * field, axis=(-2, -1), keepdims=True)
    return field * lax.rsqrt(mean_sq + 1e-06)


def chain(earlier, later):
    return (earlier[0] + later[0], jnp.exp(later[0])[:, :, None, None] * earlier[1] + later[1])


def inside_block(q_block, k_block, v_block, cumul):
    length = cumul.shape[1]
    heads = cumul.shape[2]
    places = jnp.arange(length)
    causal = places[:, None] >= places[None, :]
    group = min(8, heads)
    results = []
    for first in range(0, heads, group):
        trans = jnp.transpose(cumul[:, :, first : first + group], (0, 2, 1))
        diff = trans[:, :, :, None] - trans[:, :, None, :]
        factor = jnp.exp(jnp.where(causal[None, None, :, :], diff, -1e30))
        scores = jnp.einsum(
            "pthd,pshd->phts",
            q_block[:, :, first : first + group],
            k_block[:, :, first : first + group],
            preferred_element_type=jnp.float32,
        )
        weights = (scores * factor).astype(jnp.bfloat16)
        results.append(
            jnp.einsum(
                "phts,pshd->pthd",
                weights,
                v_block[:, :, first : first + group],
                preferred_element_type=jnp.float32,
            )
        )
    return jnp.concatenate(results, axis=2)


def per_device(
    queries,
    keys,
    values,
    prefill_decay,
    start_states,
    resident_states,
    slot_of_prompt,
    decode_queries,
    decode_keys,
    decode_values,
    decode_gate,
    decode_decay,
    norm_gain,
    out_weight,
):
    highest = lax.Precision.HIGHEST
    prompt_count, tok_len, heads, head_size = queries.shape
    local_cum = jnp.cumsum(prefill_decay, axis=1)
    running = jnp.zeros((prompt_count, heads, head_size, head_size), jnp.float32)
    result = inside_block(queries, keys, values, local_cum)
    ending = local_cum[:, -1]
    k_weighted = keys.astype(jnp.float32) * jnp.exp(ending[:, None, :] - local_cum)[:, :, :, None]
    running = jnp.exp(ending)[:, :, None, None] * running + jnp.einsum(
        "pshd,pshe->phde", k_weighted, values.astype(jnp.float32), precision=highest
    )
    total_local = local_cum[:, -1]
    blank = (jnp.zeros_like(total_local), jnp.zeros_like(running))
    before, carried = prefix((total_local, running), "ctx", chain, blank)
    decay_sum = lax.psum(total_local, "ctx")
    position_scale = jnp.exp(local_cum)
    q_part = queries.astype(jnp.float32)
    state_part = (
        lax.all_gather(start_states, "ctx", axis=1, tiled=True) * jnp.exp(before)[:, :, None, None]
        + carried
    )
    remote = (
        jnp.einsum("pthd,phde->pthe", q_part, state_part, precision=highest)
        * position_scale[:, :, :, None]
    )
    prefill_out = normalize(result + remote).astype(jnp.bfloat16)
    heads_dev = heads // lax.axis_size("ctx")
    head_start = lax.axis_index("ctx") * heads_dev
    own_total = lax.dynamic_slice_in_dim(decay_sum, head_start, heads_dev, 1)
    own_start = jnp.exp(own_total)[:, :, None, None] * start_states
    after = decay_sum - before - total_local
    term = jnp.exp(after)[:, :, None, None] * running
    own = lax.dynamic_slice_in_dim(term, head_start, heads_dev, 1) + own_start
    term = lax.dynamic_update_slice_in_dim(term, own, head_start, 1)
    summed = lax.psum_scatter(term, "ctx", scatter_dimension=1, tiled=True)
    handed = lax.all_to_all(summed, "grp", split_axis=3, concat_axis=0, tiled=True)
    slot_count = resident_states.shape[0]
    onehot = (slot_of_prompt[None, :] == jnp.arange(slot_count, dtype=jnp.int32)[:, None]).astype(
        jnp.float32
    )
    taken = jnp.sum(onehot, axis=1)
    cache = (
        jnp.einsum("sp,phde->shde", onehot, handed, precision=highest)
        + (1.0 - taken)[:, None, None, None] * resident_states
    )
    step_count = decode_queries.shape[1]
    outputs = []
    for step in range(step_count):
        k_now = decode_keys[:, step].astype(jnp.float32)
        v_now = decode_values[:, step].astype(jnp.float32)
        cache = (
            jnp.exp(decode_decay[:, step])[:, :, None, None] * cache
            + k_now[:, :, :, None] * v_now[:, :, None, :]
        )
        outputs.append(
            jnp.einsum(
                "shd,shde->she",
                decode_queries[:, step].astype(jnp.float32),
                cache,
                precision=highest,
            )
        )
    y_all = jnp.stack(outputs, axis=1)
    squares = jnp.sum(y_all * y_all, axis=(2, 3))
    totals = lax.psum(squares, ("ctx", "grp"))
    mean_sq = totals / (H * HS)
    normed = (
        y_all
        * lax.rsqrt(mean_sq + 1e-06)[:, :, None, None]
        * norm_gain
        * jax.nn.sigmoid(decode_gate.astype(jnp.float32))
    ).astype(jnp.bfloat16)
    columns = normed.shape[2] * normed.shape[3]
    flat = normed.reshape(slot_count * step_count, columns)
    weights = out_weight.reshape(columns, out_weight.shape[2])
    decoded = lax.psum_scatter(
        jnp.dot(flat, weights, preferred_element_type=jnp.float32),
        ("ctx", "grp"),
        scatter_dimension=0,
        tiled=True,
    )
    return (prefill_out, cache, decoded)


def solution(mesh):
    return jax.shard_map(
        per_device,
        mesh=mesh,
        in_specs=(
            P("grp", "ctx", None, None),
            P("grp", "ctx", None, None),
            P("grp", "ctx", None, None),
            P("grp", "ctx", None),
            P("grp", "ctx", None, None),
            P(None, "ctx", None, "grp"),
            P(),
            P(None, None, "ctx", None),
            P(None, None, "ctx", None),
            P(None, None, "ctx", "grp"),
            P(None, None, "ctx", "grp"),
            P(None, None, "ctx"),
            P("ctx", "grp"),
            P("ctx", "grp", None),
        ),
        out_specs=(
            P("grp", "ctx", None, None),
            P(None, "ctx", None, "grp"),
            P(("ctx", "grp"), None),
        ),
        check_vma=False,
    )
```

profile of v0, /device:TPU:0, one launch (start us, length us, event | category | flops | bytes accessed | tf_op | source)
XLA Modules:
  0.0 605.3 jit_solution(511486406370839602)
XLA Ops:
  8.1 1.1 reduce-window.6
  11.3 6.9 %multiply_bitcast_fusion = f32[512,32,128]{2,1,0:T(8,128)S(1)} fusion(bf16[1,512,32,128]{3,2,1,0:T(8,128)(2,1)} %param.17, f32[512,32]{1,0:T(8,128)S(1)} %bitcast.231), kind=kLoop, calls=%fused_computation.12 | loop fusion | flops 4194304 | bytes 12648448 | tf_op jit(solution)/shard_map/reshape.45
  18.2 15.3 %fusion.42 = f32[32,128,128]{2,1,0:T(8,128)} fusion(bf16[512,32,128]{2,1,0:T(8,128)(2,1)S(1)} %bitcast.228, f32[512,32,128]{2,1,0:T(8,128)S(1)} %multiply_bitcast_fusion, f32[32]{0:T(128)S(1)} %exponential_multiply_fusion), kind=kOutput, calls=%fused_computation.51 | convolution fusion | flops 3221749760 | bytes 14680192 | tf_op jit(solution)/shard_map/pshd,pshe->phde/dot_general | solution.py:88
  33.7 38.6 %psum.14 = f32[1,32]{1,0:T(1,128)S(1)} all-reduce(f32[1,32]{1,0:T(1,128)S(1)} %bitcast.246), channel_id=1, replica_groups=mesh['ctx'=16,'grp'=8] {'ctx'}, use_global_device_ids=true, to_apply=%region_5.6 | all-reduce | flops 32 | bytes 256 | tf_op jit(solution)/shard_map/psum | solution.py:94
  72.3 18.8 %all_gather.13 = f32[16,1,32]{2,1,0:T(1,128)S(1)} all-gather(f32[1,1,32]{2,1,0:T(1,128)S(1)} %copy.116), channel_id=1, replica_groups=mesh['ctx'=16,'grp'=8] {'ctx'}, dimensions={0}, use_global_device_ids=true | all-gather | bytes 2176 | tf_op jit(solution)/shard_map/all_gather | solution.py:12
  91.2 132.8 %all-gather.6.cloned.1.call-done = f32[512,128,128]{2,1,0:T(8,128)} async-done(((f32[32,128,128]{2,1,0:T(8,128)}), f32[512,128,128]{2,1,0:T(8,128)}) %all-gather.6.cloned.1.call-update) | async-done | bytes 33554448 | tf_op jit(solution)/shard_map/all_gather | solution.py:12
  224.0 34.4 %while.16 = (s32[]{:T(128)}, f32[1,32]{1,0:T(1,128)S(1)}, f32[1,32,128,128]{3,2,1,0:T(8,128)S(1)}, s32[]{:T(128)}, f32[16,1,32]{2,1,0:T(1,128)S(1)}, /*index=5*/f32[16,1,32,128,128]{4,3,2,1,0:T(8,128)}, s32[]{:T(128)}, s32[]{:T(128)}) while((s32[]{:T(128)}, f32[1,32]{1,0:T(1,128)S(1)}, f32[1,32,128,128]{3,2,1,0:T(8,128)S(1)}, ...), condition=%wide.region_3.4_spmd.clone, body=%wide.region_2.3_spmd.clone.sunk | while | flops 2097252 | bytes 6292343 | solution.py:24
  224.0 2.1 fusion.88
  226.2 2.1 fusion.88
  228.3 2.1 fusion.88
  230.5 2.1 fusion.88
  232.6 2.1 fusion.88
  234.8 2.1 fusion.88
  236.9 2.1 fusion.88
  239.1 2.1 fusion.88
  241.3 2.1 fusion.88
  243.4 2.1 fusion.88
  245.6 2.1 fusion.88
  247.7 2.1 fusion.88
  249.9 2.1 fusion.88
  252.0 2.1 fusion.88
  254.2 2.1 fusion.88
  256.3 2.1 fusion.88
  259.0 1.9 broadcast_multiply_fusion
  260.9 1.5 fusion.85
  264.6 4.1 fusion.78
  268.7 2.5 fusion.80
  276.5 2.5 copy.167
  279.0 4.5 fusion.79
  283.5 1.5 copy.164
  285.1 1.3 copy_bitcast_fusion.26
  286.4 1.3 exponential_bitcast_fusion.2
  287.7 6.9 %fusion.38 = f32[1,512,8,128]{1,3,2,0:T(8,128)} fusion(f32[8,512]{1,0:T(8,128)} %get-tuple-element.228, pred[512,512]{1,0:T(8,128)(4,1)} %iota_compare_fusion, bf16[1,512,8,128]{3,2,1,0:T(8,128)(2,1)} %get-tuple-element.200, bf16[1,512,8,128]{3,2,1,0:T(8,128)(2,1)} %get-tuple-element.196, bf16[1,512,8,128]{1,3,2,0:T(8,128)(2,1)} %copy.167), kind=kOutput, calls=%fused_computation.47 | convolution fusion | flops 1082130432 | bytes 5521408 | tf_op jit(solution)/shard_map/phts,pshd->pthd/dot_general | solution.py:55
  294.7 6.5 %fusion.39 = f32[1,512,8,128]{1,3,2,0:T(8,128)} fusion(f32[8,512]{1,0:T(8,128)} %get-tuple-element.229, pred[512,512]{1,0:T(8,128)(4,1)} %iota_compare_fusion, bf16[1,512,8,128]{3,2,1,0:T(8,128)(2,1)} %get-tuple-element.198, bf16[1,512,8,128]{3,2,1,0:T(8,128)(2,1)} %get-tuple-element.194, bf16[1,512,8,128]{1,3,2,0:T(8,128)(2,1)S(1)} %copy-done.7), kind=kOutput, calls=%fused_computation.48 | convolution fusion | flops 1082130432 | bytes 5521408 | tf_op jit(solution)/shard_map/phts,pshd->pthd/dot_general | solution.py:55
  301.2 30.5 %reduce-scatter.2.cloned.1.call-done = f32[1,2,128,128]{3,2,1,0:T(8,128)} async-done(((f32[1,32,128,128]{3,2,1,0:T(8,128)}), f32[1,2,128,128]{3,2,1,0:T(8,128)}) %reduce-scatter.2.cloned.1.call-update) | async-done | bytes 131088 | tf_op jit(solution)/shard_map/reduce_scatter | solution.py:114
  331.7 1.7 copy.124
  333.4 4.7 all-to-all-start
  338.7 6.0 all-to-all-done
  344.8 4.6 multiply_add_fusion
  350.0 1.6 fusion.63
  351.5 0.9 copy.147
  352.4 3.4 fusion.57
  355.8 1.5 copy.139
  357.3 3.4 fusion.55
  360.7 1.5 copy.142
  362.2 3.4 fusion.53
  365.6 1.5 copy.145
  367.1 1.4 multiply_reduce_fusion.1
  368.5 62.9 %psum.15 = f32[64,4]{0,1:T(4,128)} all-reduce(f32[64,4]{0,1:T(4,128)} %multiply_reduce_fusion.1), channel_id=1, replica_groups=mesh['ctx'=16,'grp'=8] {'ctx','grp'}, use_global_device_ids=true, to_apply=%region_9.10 | all-reduce | flops 256 | bytes 2048 | tf_op jit(solution)/shard_map/psum | solution.py:144
  432.0 1.5 multiply_convert_fusion.17
  433.5 1.5 copy.132
  435.0 1.7 reshape.340
  436.7 4.5 fusion.81
  441.9 1.3 copy_bitcast_fusion.28
  443.2 2.4 copy.161
  445.7 1.5 copy.158
  447.1 1.5 copy.236
  448.6 7.0 %fusion.40 = f32[1,512,8,128]{1,3,2,0:T(8,128)} fusion(f32[8,512]{1,0:T(8,128)} %get-tuple-element.230, pred[512,512]{1,0:T(8,128)(4,1)} %iota_compare_fusion, bf16[1,512,8,128]{3,2,1,0:T(8,128)(2,1)} %get-tuple-element.199, bf16[1,512,8,128]{3,2,1,0:T(8,128)(2,1)} %get-tuple-element.195, bf16[1,512,8,128]{1,3,2,0:T(8,128)(2,1)} %copy.161), kind=kOutput, calls=%fused_computation.49 | convolution fusion | flops 1082130432 | bytes 5521408 | tf_op jit(solution)/shard_map/phts,pshd->pthd/dot_general | solution.py:55
  455.6 6.6 %fusion.41 = f32[1,512,8,128]{1,3,2,0:T(8,128)} fusion(f32[8,512]{1,0:T(8,128)S(1)} %copy-done.14, pred[512,512]{1,0:T(8,128)(4,1)} %iota_compare_fusion, bf16[1,512,8,128]{3,2,1,0:T(8,128)(2,1)} %get-tuple-element.197, bf16[1,512,8,128]{3,2,1,0:T(8,128)(2,1)} %get-tuple-element.193, bf16[1,512,8,128]{1,3,2,0:T(8,128)(2,1)S(1)} %copy-done.6), kind=kOutput, calls=%fused_computation.50 | convolution fusion | flops 1082130432 | bytes 5521408 | tf_op jit(solution)/shard_map/phts,pshd->pthd/dot_general | solution.py:55
  462.2 12.9 %multiply_reduce_fusion = (f32[512]{0:T(512)S(1)}, f32[1,512,32,128]{1,3,2,0:T(8,128)}) fusion(f32[512,32]{0,1:T(8,128)} %bitcast.244, bf16[512,32,128]{2,1,0:T(8,128)(2,1)} %bitcast.229, f32[1,32,128,128]{3,2,1,0:T(8,128)S(1)} %get-tuple-element.114, f32[1,32,128,128]{3,2,0,1:T(8,128)} %all-gather.4.cloned.1.call-done, f32[32]{0:T(128)} %get-tuple-element.224, ...), kind=kOutput, calls=%fused_computation.11 | convolution fusion | flops 3236953600 | bytes 25233536 | tf_op jit(solution)/shard_map/pthd,phde->pthe/dot_general | solution.py:102
  475.1 6.7 %multiply_convert_fusion = bf16[1,512,32,128]{1,3,2,0:T(8,128)(2,1)} fusion(f32[1,512,32,128]{1,3,2,0:T(8,128)} %get-tuple-element.226, f32[512]{0:T(512)S(1)} %add_rsqrt_fusion.1), kind=kLoop, calls=%fused_computation.10 | loop fusion | flops 4194304 | bytes 12584960 | tf_op jit(solution)/shard_map/convert_element_type | solution.py:105
  481.8 7.9 %copy.133 = bf16[1,512,32,128]{3,2,1,0:T(8,128)(2,1)} copy(bf16[1,512,32,128]{1,3,2,0:T(8,128)(2,1)} %multiply_convert_fusion) | data formatting | bytes 8388608
  489.7 107.1 %all-reduce.3.cloned.1.call-done = f32[256,6144]{1,0:T(8,128)} async-done(((f32[256,6144]{1,0:T(8,128)}), f32[256,6144]{1,0:T(8,128)}) %all-reduce.3.cloned.1.call-update) | async-done | bytes 6291472
  596.7 1.6 constant_dynamic-slice_fusion.2
  (105 shorter events, 14.2 us)
Async XLA Ops:
  7.2 429.5 %copy-start = (bf16[2,16,6144]{2,1,0:T(8,128)(2,1)S(1)}, bf16[2,16,6144]{2,1,0:T(8,128)(2,1)}, u32[]{:S(2)}) copy-start(bf16[2,16,6144]{2,1,0:T(8,128)(2,1)} %param.29) | copy-start | bytes 1179652
  7.2 216.8 %all-gather.6.cloned.1.call-start = ((), (), s32[]{:S(2)}) async-start(), calls=%async_computation.4 | async-start | bytes 35651584 | tf_op jit(solution)/shard_map/all_gather | solution.py:12
  11.3 7.0 %copy-start.2 = (bf16[1,512,32,128]{3,2,1,0:T(8,128)(2,1)S(1)}, bf16[1,512,32,128]{3,2,1,0:T(8,128)(2,1)}, u32[]{:S(2)}) copy-start(bf16[1,512,32,128]{3,2,1,0:T(8,128)(2,1)} %param.18) | copy-start | bytes 12582916
  33.6 298.2 %reduce-scatter.2.cloned.1.call-start = ((), (), s32[]{:S(2)}) async-start(), calls=%async_computation.3 | async-start | bytes 2228224 | tf_op jit(solution)/shard_map/reduce_scatter | solution.py:114
  258.5 2.4 copy-start.1
  259.0 3.5 copy-start.8
  263.2 199.0 %all-gather.4.cloned.1.call-start = ((), (), s32[]{:S(2)}) async-start(), calls=%async_computation.2 | async-start | bytes 2228224 | tf_op jit(solution)/shard_map/all_gather | solution.py:98
  264.6 4.1 copy-start.3
  268.7 3.3 copy-start.10
  268.7 5.9 copy-start.13
  268.7 6.5 %copy-start.15 = (s32[8]{0:T(128)S(1)}, s32[8]{0:T(128)}, u32[]{:S(2)}) copy-start(s32[8]{0:T(128)} %param.22) | copy-start | bytes 100
  268.7 7.1 %copy-start.11 = (bf16[64,4,2,128]{3,2,1,0:T(2,128)(2,1)S(1)}, bf16[64,4,2,128]{3,2,1,0:T(2,128)(2,1)}, u32[]{:S(2)}) copy-start(bf16[64,4,2,128]{3,2,1,0:T(2,128)(2,1)} %param.23) | copy-start | bytes 393220
  287.7 6.9 %copy-start.7 = (bf16[1,512,8,128]{1,3,2,0:T(8,128)(2,1)S(1)}, bf16[1,512,8,128]{1,3,2,0:T(8,128)(2,1)}, u32[]{:S(2)}) copy-start(bf16[1,512,8,128]{1,3,2,0:T(8,128)(2,1)} %copy.164) | copy-start | bytes 3145732
  333.4 11.4 %all-to-all-start = ((f32[1,2,128,128]{2,1,0,3:T(2,128)}), f32[1,2,128,128]{2,1,0,3:T(2,128)S(1)}, u32[]{:S(2)}, u32[]{:S(2)}) async-start(f32[1,2,128,128]{2,1,0,3:T(2,128)} %copy.124), calls=%async_computation.1 | async-start | bytes 262144 | tf_op jit(solution)/shard_map/all_to_all | solution.py:115
  338.1 258.7 %all-reduce.3.cloned.1.call-start = ((), (), s32[]{:S(2)}) async-start(), calls=%async_computation.5 | async-start | bytes 12582912
  344.8 5.2 copy-start.9
  349.9 91.2 %copy-start.4 = (f32[64,2,128,16]{2,3,1,0:T(8,128)}, f32[64,2,128,16]{2,3,1,0:T(8,128)S(1)}, u32[]{:S(2)}) copy-start(f32[64,2,128,16]{2,3,1,0:T(8,128)S(1)} %copy.134) | copy-start | bytes 3145732
  441.2 0.7 copy-start.12
  441.2 4.5 copy-start.5
  448.6 7.0 %copy-start.6 = (bf16[1,512,8,128]{1,3,2,0:T(8,128)(2,1)S(1)}, bf16[1,512,8,128]{1,3,2,0:T(8,128)(2,1)}, u32[]{:S(2)}) copy-start(bf16[1,512,8,128]{1,3,2,0:T(8,128)(2,1)} %copy.158) | copy-start | bytes 3145732
  448.6 7.0 %copy-start.14 = (f32[8,512]{1,0:T(8,128)S(1)}, f32[8,512]{1,0:T(8,128)}, u32[]{:S(2)}) copy-start(f32[8,512]{1,0:T(8,128)} %get-tuple-element.231) | copy-start | bytes 49156
Sparse Core Ops, SparseCore 0:
  33.7 190.2 all-gather.5
  263.3 68.3 reduce-scatter.1
  334.2 47.5 all-gather.3
  441.3 155.3 all-reduce.2
where the time goes:
time: 617 us; the launch traced here: 605 us
  waiting for transfers between devices  277 us (45%)
  blocking collectives  120 us (19%)
  matrix products  76 us (12%)
  other arithmetic  60.5 us (10%)
  local copies, waits for them, and re-layouts  51.6 us (8%)
  between operations  14.5 us (2%)
    all_gather x1, waiting for transfers between devices, prefix(): everything = jax.tree.map(lambda part: lax.all_gather(part, axis), array)  133 us
    unnamed x5, waiting for transfers between devices  108 us
    psum x1, blocking collectives, per_device(): totals = lax.psum(squares, ('ctx', 'grp'))  62.9 us
    psum x1, blocking collectives, per_device(): decay_sum = lax.psum(total_local, 'ctx')  38.6 us
    select_n x32, other arithmetic, step(): return jax.tree.map(lambda a, b: jnp.where(reached, a, b), new, before)  33.8 us
    reduce_scatter x1, waiting for transfers between devices, per_device(): summed = lax.psum_scatter(term, 'ctx', scatter_dimension=1, tiled=True)  30.5 us
    dot_general x4, matrix products, inside_block(): jnp.einsum('phts,pshd->pthd', weights, v_block[:, :, first:first + group]...  27 us
    unnamed x42, local copies, waits for them, and re-layouts  22.9 us
  transfers between devices with their start and end apart: 5, of which 4 were waited for; matrix products, arithmetic and copies ran while one was open for 20% of the time, Pallas kernels for 0%

commit v1 on v0

v1 whole, which is shorter than its diff:
```python
import jax
import jax.numpy as jnp
from jax import lax
from jax.experimental import pallas as pl
from jax.experimental.pallas import tpu as pltpu
from jax.sharding import PartitionSpec as P

H = 32
HS = 128
LOG2E = 1.4426950408889634
MESH = pl.DeviceIdType.MESH
F32 = jnp.float32
BF16 = jnp.bfloat16
VMEM_LIMIT = 60 * 1024 * 1024
T = 512
CH = 128
ROWS = 136
FIRST_HEADS = 16


def dot(a, b):
    return lax.dot_general(a, b, (((1,), (0,)), ((), ())), preferred_element_type=F32)


def split(x):
    hi = x.astype(BF16)
    return hi, (x - hi.astype(F32)).astype(BF16)


def head_of(half, i):
    return 4 * lax.div(i, 2) + 2 * half + lax.rem(i, 2)


def remote(src, dst, send, recv, where):
    return pltpu.make_async_remote_copy(
        src_ref=src, dst_ref=dst, send_sem=send, recv_sem=recv, device_id=where, device_id_type=MESH
    )


def prefill_kernel(
    q_hbm, k_hbm, v_hbm, dec_ref, start_ref, w_ref,
    att_hbm, qh_hbm, p_ref, hand_ref, wt_ref, ec_ref,
    raw, stage, qh, kt, vh, cum2, cum, s_ref, xbuf, tbuf, rbuf, pbuf, qbuf, obuf, pcur, fbuf, hbuf, wf, wr, abuf,
    load_sem, q_sem, att_sem, sa, ra, s1, r1, s2, r2, sb, rb, sh, rh, sw, rw,
):
    c, g = lax.axis_index("ctx"), lax.axis_index("grp")
    core, chip = lax.rem(c, 2), lax.div(c, 2)
    other = 1 - core
    partner = (2 * chip + other, g)

    def peer(j):
        return (2 * j + core, g)

    def load(which, hbm, at):
        return pltpu.make_async_copy(
            hbm.at[pl.ds(at * CH, CH)], raw.at[which, pl.ds(at * CH, CH)], load_sem.at[which, at]
        )

    for which, hbm in ((0, k_hbm), (1, v_hbm), (2, q_hbm)):
        for at in range(T // CH):
            load(which, hbm, at).start()

    bar = pltpu.get_barrier_semaphore()
    pl.semaphore_signal(bar, inc=1, device_id=partner, device_id_type=MESH)

    def greet(d, _):
        pl.semaphore_signal(bar, inc=1, device_id=peer(lax.rem(chip + d, 8)), device_id_type=MESH)
        pl.semaphore_signal(bar, inc=1, device_id=(c, lax.rem(g + d, 8)), device_id_type=MESH)
        return 0

    lax.fori_loop(1, 8, greet, 0)

    lane = lax.broadcasted_iota(jnp.int32, (H, T), 1)
    x = dec_ref[...]
    step = 1
    while step < T:
        x = x + jnp.where(lane >= step, pltpu.roll(x, step, 1), 0.0)
        step *= 2
    cum[...] = x
    cum2[...] = x * LOG2E
    ec_ref[...] = jnp.concatenate([jnp.exp(x), jnp.zeros((HS - H, T), F32)], axis=0).T

    def relay(which, hbm, at, put):
        load(which, hbm, at).wait()
        stage[...] = raw[which, pl.ds(at * CH, CH)].astype(F32).reshape(CH * H, HS)
        for h in range(H):
            put(h, pl.ds(pl.multiple_of(at * CH, CH), CH), stage[pl.ds(h, CH, stride=H), :])

    def put_k(h, span, block):
        kt[h, :, span] = block.T.astype(BF16)

    def put_v(h, span, block):
        vh[h, span, :] = block.astype(BF16)

    def put_q(h, span, block):
        qh[h, span, :] = block.astype(BF16)

    def relay_kv(at, _):
        relay(0, k_hbm, at, put_k)
        relay(1, v_hbm, at, put_v)
        return 0

    lax.fori_loop(0, T // CH, relay_kv, 0)

    def local_state(half, i):
        h = head_of(half, i)
        row = cum[pl.ds(h, 1), :]
        end = row[:, T - 1 : T]
        hi, lo = split(kt[h].astype(F32) * jnp.exp(end - row))
        both = dot(jnp.concatenate([hi, lo], axis=0), vh[h])
        s_ref[half, i, 0:HS, :] = both[:HS] + both[HS:]
        s_ref[half, i, HS:ROWS, :] = jnp.broadcast_to(end, (ROWS - HS, HS))

    def copy_a(m):
        return remote(s_ref.at[other, pl.ds(4 * m, 4)], xbuf.at[pl.ds(4 * m, 4)], sa.at[m], ra.at[m], partner)

    pl.semaphore_wait(bar, 15)

    def other_half(m, _):
        def one(i, _):
            local_state(other, 4 * m + i)
            return 0

        lax.fori_loop(0, 4, one, 0)
        copy_a(m).start()
        return 0

    lax.fori_loop(0, 4, other_half, 0)

    def own_half(i, _):
        local_state(core, i)
        return 0

    lax.fori_loop(0, 16, own_half, 0)

    def wait_a(m, _):
        copy_a(m).wait_recv()
        return 0

    lax.fori_loop(0, 4, wait_a, 0)

    def copy_1(j):
        return remote(tbuf.at[j], rbuf.at[chip], s1.at[j], r1.at[chip], peer(j))

    def arrival_1(j):
        return remote(tbuf.at[j], rbuf.at[j], s1.at[j], r1.at[j], peer(j))

    def chip_total(j):
        for r in range(2):
            i = 2 * j + r
            mine, theirs = s_ref[core, i], xbuf[i]
            end_mine, end_theirs = mine[HS : HS + 1], theirs[HS : HS + 1]
            on_mine = jnp.where(core == 0, jnp.exp(end_theirs), 1.0)
            on_theirs = jnp.where(core == 0, 1.0, jnp.exp(end_mine))
            tbuf[j, r, 0:HS, :] = on_mine * mine[:HS] + on_theirs * theirs[:HS]
            tbuf[j, r, HS:ROWS, :] = mine[HS:] + theirs[HS:]

    def send_total(d, _):
        j = lax.rem(chip + d, 8)
        chip_total(j)
        copy_1(j).start()
        return 0

    lax.fori_loop(1, 8, send_total, 0)
    chip_total(chip)
    rbuf[chip] = tbuf[chip]

    for to in range(8):
        wf[to] = w_ref[:, to * 768 : (to + 1) * 768].astype(F32)

    def copy_w(to):
        return remote(wf.at[to], wr.at[g], sw.at[to], rw.at[g], (c, to))

    def arrival_w(frm):
        return remote(wf.at[frm], wr.at[frm], sw.at[frm], rw.at[frm], (c, frm))

    def send_w(d, _):
        copy_w(lax.rem(g + d, 8)).start()
        return 0

    lax.fori_loop(1, 8, send_w, 0)
    wr[g] = wf[g]

    def relay_q(at, _):
        relay(2, q_hbm, at, put_q)
        return 0

    lax.fori_loop(0, T // CH, relay_q, 0)
    qh_copy = pltpu.make_async_copy(qh, qh_hbm, q_sem)
    qh_copy.start()

    causal = lax.broadcasted_iota(jnp.int32, (HS, HS), 0) >= lax.broadcasted_iota(jnp.int32, (HS, HS), 1)

    def att_copy(h, slot):
        return pltpu.make_async_copy(abuf.at[slot], att_hbm.at[h], att_sem.at[slot])

    def attend(h, slot):
        row = cum2[pl.ds(h, 1), :]
        col = jnp.broadcast_to(row, (HS, T)).T
        left = dot(qh[h], kt[h, :, 0:256])
        right = dot(qh[h, 256:512, :], kt[h, :, 256:512])

        def weigh(a, b):
            scores = left if b < 2 else right
            first = a if b < 2 else a - 2
            part = scores[first * HS : (first + 1) * HS, (b % 2) * HS : (b % 2 + 1) * HS]
            diff = col[a * HS : (a + 1) * HS] - row[:, b * HS : (b + 1) * HS]
            if a == b:
                diff = jnp.where(causal, diff, -1e30)
            return (part * jnp.exp2(diff)).astype(BF16)

        v = vh[h]
        none = jnp.zeros((HS, HS), BF16)
        top = jnp.concatenate([
            jnp.concatenate([weigh(0, 0), none], axis=1),
            jnp.concatenate([weigh(1, 0), weigh(1, 1)], axis=1),
        ], axis=0)
        low = jnp.concatenate([
            jnp.concatenate([weigh(2, 0), weigh(2, 1), weigh(2, 2), none], axis=1),
            jnp.concatenate([weigh(3, 0), weigh(3, 1), weigh(3, 2), weigh(3, 3)], axis=1),
        ], axis=0)
        abuf[slot, 0:256, :] = dot(top, v[0:256])
        abuf[slot, 256:512, :] = dot(low, v)

    def pair(n, _):
        for slot in range(2):

            @pl.when(n > 0)
            def _():
                att_copy(2 * n - 2 + slot, slot).wait()

            attend(2 * n + slot, slot)
            att_copy(2 * n + slot, slot).start()
        return 0

    lax.fori_loop(0, FIRST_HEADS // 2, pair, 0)

    def copy_2(j):
        return remote(pbuf.at[j], qbuf.at[chip], s2.at[j], r2.at[chip], peer(j))

    def arrival_2(j):
        return remote(pbuf.at[j], qbuf.at[j], s2.at[j], r2.at[j], peer(j))

    pcur[...] = start_ref[...]

    def scan(j, _):
        pbuf[j] = pcur[...]

        @pl.when(j != chip)
        def _():
            copy_2(j).start()
            arrival_1(j).wait_recv()

        for r in range(2):
            pcur[r] = jnp.exp(rbuf[j, r, HS : HS + 1, :]) * pcur[r] + rbuf[j, r, 0:HS, :]
        return 0

    lax.fori_loop(0, 8, scan, 0)
    qbuf[chip] = pbuf[chip]

    for r in range(2):
        fbuf[:, r] = pcur[r].T.reshape(8, 16, HS)

    def copy_h(to):
        return remote(fbuf.at[to], hbuf.at[g], sh.at[to], rh.at[g], (c, to))

    def arrival_h(frm):
        return remote(fbuf.at[frm], hbuf.at[frm], sh.at[frm], rh.at[frm], (c, frm))

    def send_h(d, _):
        copy_h(lax.rem(g + d, 8)).start()
        return 0

    lax.fori_loop(1, 8, send_h, 0)
    hbuf[g] = fbuf[g]

    lax.fori_loop(FIRST_HEADS // 2, H // 2, pair, 0)

    def copy_b(m):
        return remote(obuf.at[pl.ds(4 * m, 4)], p_ref.at[core, pl.ds(4 * m, 4)], sb.at[m], rb.at[m], partner)

    def arrival_b(m):
        return remote(obuf.at[pl.ds(4 * m, 4)], p_ref.at[other, pl.ds(4 * m, 4)], sb.at[m], rb.at[m], partner)

    def spread(m, _):
        for n in range(2):
            j = 2 * m + n

            @pl.when(j != chip)
            def _():
                arrival_2(j).wait_recv()

            for r in range(2):
                i = 2 * j + r
                before = qbuf[j, r]
                first = jnp.where(core == 0, s_ref[core, i], xbuf[i])
                after = jnp.exp(first[HS : HS + 1]) * before + first[:HS]
                p_ref[core, i] = jnp.where(core == 0, before, after)
                obuf[i] = jnp.where(core == 0, after, before)
        copy_b(m).start()
        return 0

    lax.fori_loop(0, 4, spread, 0)

    def take_w(d, _):
        frm = lax.rem(g + d, 8)
        arrival_w(frm).wait_recv()
        arrival_h(frm).wait_recv()
        return 0

    lax.fori_loop(1, 8, take_w, 0)
    for frm in range(8):
        wt_ref[frm * 32 : (frm + 1) * 32, :] = wr[frm].astype(BF16)
    hand_ref[...] = hbuf[...]

    for slot in range(2):
        att_copy(H - 2 + slot, slot).wait()
    qh_copy.wait()

    def finish_pair(m, _):
        arrival_b(m).wait_recv()
        copy_b(m).wait_send()
        copy_a(m).wait_send()
        return 0

    lax.fori_loop(0, 4, finish_pair, 0)

    def finish(d, _):
        j = lax.rem(chip + d, 8)
        copy_1(j).wait_send()
        copy_2(j).wait_send()
        to = lax.rem(g + d, 8)
        copy_w(to).wait_send()
        copy_h(to).wait_send()
        return 0

    lax.fori_loop(1, 8, finish, 0)


def prefill(q, k, v, decay, start, weight):
    dma = pltpu.SemaphoreType.DMA
    anywhere = pl.BlockSpec(memory_space=pl.ANY)
    vmem = pl.BlockSpec(memory_space=pltpu.VMEM)
    return pl.pallas_call(
        prefill_kernel,
        name="prefill",
        out_shape=(
            jax.ShapeDtypeStruct((H, T, HS), F32),
            jax.ShapeDtypeStruct((H, T, HS), BF16),
            jax.ShapeDtypeStruct((2, 16, HS, HS), F32),
            jax.ShapeDtypeStruct((8, 2, 16, HS), F32),
            jax.ShapeDtypeStruct((256, 768), BF16),
            jax.ShapeDtypeStruct((T, HS), F32),
        ),
        in_specs=[anywhere, anywhere, anywhere, vmem, vmem, vmem],
        out_specs=(anywhere, anywhere, vmem, vmem, vmem, vmem),
        scratch_shapes=[
            pltpu.VMEM((3, T, H, HS), BF16),
            pltpu.VMEM((CH * H, HS), F32),
            pltpu.VMEM((H, T, HS), BF16),
            pltpu.VMEM((H, HS, T), BF16),
            pltpu.VMEM((H, T, HS), BF16),
            pltpu.VMEM((H, T), F32),
            pltpu.VMEM((H, T), F32),
            pltpu.VMEM((2, 16, ROWS, HS), F32),
            pltpu.VMEM((16, ROWS, HS), F32),
            pltpu.VMEM((8, 2, ROWS, HS), F32),
            pltpu.VMEM((8, 2, ROWS, HS), F32),
            pltpu.VMEM((8, 2, HS, HS), F32),
            pltpu.VMEM((8, 2, HS, HS), F32),
            pltpu.VMEM((16, HS, HS), F32),
            pltpu.VMEM((2, HS, HS), F32),
            pltpu.VMEM((8, 2, 16, HS), F32),
            pltpu.VMEM((8, 2, 16, HS), F32),
            pltpu.VMEM((8, 32, 768), F32),
            pltpu.VMEM((8, 32, 768), F32),
            pltpu.VMEM((2, T, HS), F32),
            dma((3, T // CH)), dma, dma((2,)),
            dma((4,)), dma((4,)), dma((8,)), dma((8,)), dma((8,)), dma((8,)),
            dma((4,)), dma((4,)), dma((8,)), dma((8,)), dma((8,)), dma((8,)),
        ],
        compiler_params=pltpu.CompilerParams(
            collective_id=0, has_side_effects=True, vmem_limit_bytes=VMEM_LIMIT
        ),
    )(q, k, v, decay, start, weight)


def finish_kernel(att_ref, q_ref, p_ref, ec_ref, out_ref, wide, field, stage):
    @pl.when(pl.program_id(0) == 0)
    def _():
        for h in range(H):
            hi, lo = split(p_ref[(h // 2) % 2, 2 * (h // 4) + h % 2])
            wide[h, :, 0:HS] = hi
            wide[h, :, HS:] = lo

    squares = jnp.zeros((CH, HS), F32)
    for h in range(H):
        both = dot(q_ref[h], wide[h])
        x = att_ref[h] + (both[:, :HS] + both[:, HS:]) * ec_ref[:, h : h + 1]
        field[h] = x
        squares = squares + x * x
    mean = jnp.sum(squares, axis=1, keepdims=True) / (H * HS)
    scale = jnp.broadcast_to(lax.rsqrt(mean + 1e-06), (CH, HS))
    for h in range(H):
        stage[pl.ds(h, CH, stride=H), :] = field[h] * scale
    out_ref[...] = stage[...].reshape(CH, H, HS).astype(BF16)


def finish(att, qh, states, ec):
    return pl.pallas_call(
        finish_kernel,
        name="finish",
        grid=(T // CH,),
        out_shape=jax.ShapeDtypeStruct((T, H, HS), BF16),
        in_specs=[
            pl.BlockSpec((H, CH, HS), lambda i: (0, i, 0)),
            pl.BlockSpec((H, CH, HS), lambda i: (0, i, 0)),
            pl.BlockSpec((2, 16, HS, HS), lambda i: (0, 0, 0, 0)),
            pl.BlockSpec((CH, HS), lambda i: (i, 0)),
        ],
        out_specs=pl.BlockSpec((CH, H, HS), lambda i: (i, 0, 0)),
        scratch_shapes=[
            pltpu.VMEM((H, HS, 2 * HS), BF16),
            pltpu.VMEM((H, CH, HS), F32),
            pltpu.VMEM((CH * H, HS), F32),
        ],
        compiler_params=pltpu.CompilerParams(vmem_limit_bytes=VMEM_LIMIT),
    )(att, qh, states, ec)


def decode_kernel(
    slot_ref, cache_in, hand_ref, q_ref, k_ref, v_ref, gate_ref, decay_ref, gain_ref,
    cache_ref, z_ref, rows,
):
    cache_ref[...] = cache_in[...]
    for p in range(8):
        cache_ref[slot_ref[p]] = hand_ref[p]
    lane = lax.broadcasted_iota(jnp.int32, (16, 64), 1)
    pick = lax.broadcasted_iota(jnp.int32, (8, 64), 1)
    scale = jnp.exp(decay_ref[...])

    def one(s, ys):
        here = lane == s
        q, k = q_ref[s].astype(F32), k_ref[s].astype(F32)
        factor = jnp.sum(jnp.where(pick == s, scale, 0.0), axis=1, keepdims=True)
        ys = list(ys)
        for h in range(2):
            state = cache_ref[s, h]
            for i in range(4):
                value = jnp.sum(jnp.where(here, v_ref[i, h].astype(F32), 0.0), axis=1, keepdims=True)
                state = factor[2 * i + h : 2 * i + h + 1] * state + value * k[i, h : h + 1, :]
                y = jnp.sum(state * q[i, h : h + 1, :], axis=1, keepdims=True)
                ys[2 * i + h] = jnp.where(here, y, ys[2 * i + h])
            cache_ref[s, h] = state
        return tuple(ys)

    ys = lax.fori_loop(0, 64, one, tuple(jnp.zeros((16, 64), F32) for _ in range(8)), unroll=2)
    for i in range(4):
        squares = jnp.zeros((1, 64), F32)
        parts = []
        for h in range(2):
            y = ys[2 * i + h]
            squares = squares + jnp.sum(y * y, axis=0, keepdims=True)
            parts.append(y * gain_ref[h] * jax.nn.sigmoid(gate_ref[i, h].astype(F32)))
        parts.append(jnp.broadcast_to(squares, (8, 64)))
        parts.append(jnp.zeros((HS - 40, 64), F32))
        rows[pl.ds(i, 64, stride=4), :] = jnp.concatenate(parts, axis=0).T
    z_ref[...] = rows[...].T[:40]


def decode(slot, cache, hand, q, k, v, gate, decay, gain):
    vmem = pl.BlockSpec(memory_space=pltpu.VMEM)
    return pl.pallas_call(
        decode_kernel,
        name="decode",
        out_shape=(
            jax.ShapeDtypeStruct((64, 2, 16, HS), F32),
            jax.ShapeDtypeStruct((40, 256), F32),
        ),
        in_specs=[pl.BlockSpec(memory_space=pltpu.SMEM)] + [vmem] * 8,
        out_specs=(vmem, vmem),
        scratch_shapes=[pltpu.VMEM((256, HS), F32)],
        compiler_params=pltpu.CompilerParams(vmem_limit_bytes=VMEM_LIMIT),
    )(slot, cache, hand, q, k, v, gate, decay, gain)


def project_kernel(z_ref, w_ref, out_ref, zbuf, part, take, done, last, s1, r1, s2, r2, s3, r3):
    c, g = lax.axis_index("ctx"), lax.axis_index("grp")
    bar = pltpu.get_barrier_semaphore()

    def greet_grp(d, _):
        pl.semaphore_signal(bar, inc=1, device_id=(c, lax.rem(g + d, 8)), device_id_type=MESH)
        return 0

    def greet_ctx(d, _):
        pl.semaphore_signal(bar, inc=1, device_id=(lax.rem(c + d, 16), g), device_id_type=MESH)
        return 0

    lax.fori_loop(1, 8, greet_grp, 0)
    lax.fori_loop(1, 16, greet_ctx, 0)
    pl.semaphore_wait(bar, 22)

    def copy_1(to):
        return remote(z_ref, zbuf.at[g], s1.at[to], r1.at[g], (c, to))

    def arrival_1(frm):
        return remote(z_ref, zbuf.at[frm], s1.at[frm], r1.at[frm], (c, frm))

    def send_1(d, _):
        copy_1(lax.rem(g + d, 8)).start()
        return 0

    lax.fori_loop(1, 8, send_1, 0)
    zbuf[g] = z_ref[...]

    def wait_1(d, _):
        arrival_1(lax.rem(g + d, 8)).wait_recv()
        return 0

    lax.fori_loop(1, 8, wait_1, 0)

    z = jnp.concatenate([zbuf[n, 0:32, :] for n in range(8)], axis=0).T
    squares = zbuf[0, 32:40, :]
    for n in range(1, 8):
        squares = squares + zbuf[n, 32:40, :]
    squares = jnp.concatenate([squares] * 16, axis=0).T
    hi, lo = split(z)
    for n in range(3):
        span = slice(n * 256, (n + 1) * 256)
        w = w_ref[:, span]
        part[:, :, span] = (dot(hi, w) + dot(lo, w)).reshape(16, 16, 256)
    part[:, :, 768:896] = squares.reshape(16, 16, HS)

    def copy_2(to):
        return remote(part.at[to], take.at[c], s2.at[to], r2.at[c], (to, g))

    def arrival_2(frm):
        return remote(part.at[frm], take.at[frm], s2.at[frm], r2.at[frm], (frm, g))

    def send_2(d, _):
        copy_2(lax.rem(c + d, 16)).start()
        return 0

    lax.fori_loop(1, 16, send_2, 0)
    take[c] = part[c]

    def wait_2(d, _):
        arrival_2(lax.rem(c + d, 16)).wait_recv()
        return 0

    lax.fori_loop(1, 16, wait_2, 0)
    total = take[0]
    for n in range(1, 16):
        total = total + take[n]
    scale = lax.rsqrt(total[:, 768:769] / (H * HS) + 1e-06)
    total = total[:, :768] * scale
    for n in range(8):
        done[n] = total[2 * n : 2 * n + 2]

    def copy_3(to):
        return remote(done.at[to], last.at[g], s3.at[to], r3.at[g], (c, to))

    def arrival_3(frm):
        return remote(done.at[frm], last.at[frm], s3.at[frm], r3.at[frm], (c, frm))

    def send_3(d, _):
        copy_3(lax.rem(g + d, 8)).start()
        return 0

    lax.fori_loop(1, 8, send_3, 0)
    last[g] = done[g]

    def wait_3(d, _):
        arrival_3(lax.rem(g + d, 8)).wait_recv()
        return 0

    lax.fori_loop(1, 8, wait_3, 0)
    for n in range(8):
        out_ref[:, n * 768 : (n + 1) * 768] = last[n]

    def end_grp(d, _):
        to = lax.rem(g + d, 8)
        copy_1(to).wait_send()
        copy_3(to).wait_send()
        return 0

    def end_ctx(d, _):
        copy_2(lax.rem(c + d, 16)).wait_send()
        return 0

    lax.fori_loop(1, 8, end_grp, 0)
    lax.fori_loop(1, 16, end_ctx, 0)


def project(z, weight):
    dma = pltpu.SemaphoreType.DMA
    vmem = pl.BlockSpec(memory_space=pltpu.VMEM)
    return pl.pallas_call(
        project_kernel,
        name="project",
        out_shape=jax.ShapeDtypeStruct((2, 6144), F32),
        in_specs=[vmem, vmem],
        out_specs=vmem,
        scratch_shapes=[
            pltpu.VMEM((8, 40, 256), F32),
            pltpu.VMEM((16, 16, 896), F32),
            pltpu.VMEM((16, 16, 896), F32),
            pltpu.VMEM((8, 2, 768), F32),
            pltpu.VMEM((8, 2, 768), F32),
            dma((8,)), dma((8,)), dma((16,)), dma((16,)), dma((8,)), dma((8,)),
        ],
        compiler_params=pltpu.CompilerParams(
            collective_id=1, has_side_effects=True, vmem_limit_bytes=VMEM_LIMIT
        ),
    )(z, weight)


def per_device(
    queries, keys, values, prefill_decay, start_states, resident_states, slot_of_prompt,
    decode_queries, decode_keys, decode_values, decode_gate, decode_decay, norm_gain, out_weight,
):
    att, qh, states, hand, weight, ec = prefill(
        queries[0],
        keys[0],
        values[0],
        jnp.swapaxes(prefill_decay[0], 0, 1),
        start_states[0],
        out_weight.reshape(32, 6144),
    )
    cache, z = decode(
        slot_of_prompt,
        jnp.swapaxes(resident_states, 2, 3),
        hand,
        decode_queries,
        decode_keys,
        jnp.transpose(decode_values, (1, 2, 3, 0)),
        jnp.transpose(decode_gate, (1, 2, 3, 0)),
        jnp.transpose(decode_decay, (1, 2, 0)).reshape(8, 64),
        norm_gain[:, :, None],
    )
    decoded = project(z, weight)
    prefill_out = finish(att, qh, states, ec)
    return prefill_out[None], jnp.swapaxes(cache, 2, 3), decoded


def solution(mesh):
    return jax.shard_map(
        per_device,
        mesh=mesh,
        in_specs=(
            P("grp", "ctx", None, None),
            P("grp", "ctx", None, None),
            P("grp", "ctx", None, None),
            P("grp", "ctx", None),
            P("grp", "ctx", None, None),
            P(None, "ctx", None, "grp"),
            P(),
            P(None, None, "ctx", None),
            P(None, None, "ctx", None),
            P(None, None, "ctx", "grp"),
            P(None, None, "ctx", "grp"),
            P(None, None, "ctx"),
            P("ctx", "grp"),
            P("ctx", "grp", None),
        ),
        out_specs=(
            P("grp", "ctx", None, None),
            P(None, "ctx", None, "grp"),
            P(("ctx", "grp"), None),
        ),
        check_vma=False,
    )
```

time: 617 us -> 121 us (0.20); the launches traced: 605 us -> 120 us
  waiting for transfers between devices: 277 us -> 0 us
  blocking collectives: 120 us -> 0 us
  Pallas kernels: 0 us -> 117 us
  matrix products: 76 us -> 0 us
  other arithmetic: 60.5 us -> 0 us
  local copies, waits for them, and re-layouts: 51.6 us -> 2.12 us
  between operations: 14.5 us -> 0.66 us
    all_gather x2 -> x0, waiting for transfers between devices: 133 us -> none  [the longest x1 133 us: prefix(): everything = jax.tree.map(lambda part: lax.all_gather(part, axis), array)]
    pallas_call x0 -> x4, Pallas kernels: none -> 117 us  [the longest x1 65.6 us: prefill(): pl.pallas_call(prefill_kernel, name='prefill', out_shape=(jax.ShapeDtypeS...]
    unnamed x5 -> x0, waiting for transfers between devices: 108 us -> none
    psum x2 -> x0, blocking collectives: 101 us -> none  [the longest x1 62.9 us: per_device(): totals = lax.psum(squares, ('ctx', 'grp'))]
    dot_general x12 -> x0, matrix products: 76 us -> none  [the longest x4 27 us: inside_block(): jnp.einsum('phts,pshd->pthd', weights, v_block[:, :, first:first + group]...]
    select_n x32 -> x0, other arithmetic: 33.8 us -> none  [step(): return jax.tree.map(lambda a, b: jnp.where(reached, a, b), new, before)]
    reduce_scatter x1 -> x0, waiting for transfers between devices: 30.5 us -> none  [per_device(): summed = lax.psum_scatter(term, 'ctx', scatter_dimension=1, tiled=True)]
    unnamed x42 -> x3, local copies, waits for them, and re-layouts: 22.9 us -> 1.43 us
  transfers between devices with their start and end apart: 5 -> 0, of which waited for: 4 -> 0; matrix products, arithmetic and copies ran while one was open for 20% -> 0% of each run, Pallas kernels for 0% -> 0%
where the time goes in v1:
time: 121 us; the launch traced here: 120 us
  Pallas kernels  117 us (97%)
  local copies, waits for them, and re-layouts  2.12 us (2%)
    pallas_call x1, Pallas kernels, prefill(): pl.pallas_call(prefill_kernel, name='prefill', out_shape=(jax.ShapeDtypeS...  65.6 us
    pallas_call x1, Pallas kernels, project(): pl.pallas_call(project_kernel, name='project', out_shape=jax.ShapeDtypeSt...  30 us
    pallas_call x1, Pallas kernels, finish(): pl.pallas_call(finish_kernel, name='finish', grid=(T // CH,), out_shape=j...  12.8 us
    pallas_call x1, Pallas kernels, decode(): pl.pallas_call(decode_kernel, name='decode', out_shape=(jax.ShapeDtypeStr...  8.48 us

profile of v1, /device:TPU:0, one launch (start us, length us, event | category | flops | bytes accessed | tf_op | source)
XLA Modules:
  0.0 119.7 jit_solution(10047704320488375672)
XLA Ops:
  0.6 65.6 %prefill.1 = (f32[32,512,128]{2,1,0:T(8,128)}, bf16[32,512,128]{2,1,0:T(8,128)(2,1)}, f32[2,16,128,128]{3,2,1,0:T(8,128)}, f32[8,2,16,128]{3,2,1,0:T(8,128)}, bf...) custom-call(bf16[512,32,128]{2,1,0:T(8,128)(2,1)} %bitcast.17, bf16[512,32,128]{2,1,0:T(8,128)(2,1)} %bitcast.18, ...), custom_call_target="tpu_custom_call" | custom-call | tf_op jit(solution)/shard_map/prefill/pallas_call | solution.py:344
  66.3 0.0 copy-start
  66.3 12.8 %finish.1 = bf16[512,32,128]{2,1,0:T(8,128)(2,1)} custom-call(f32[32,512,128]{2,1,0:T(8,128)} %get-tuple-element.11.att_ref, bf16[32,512,128]{2,1,0:T(8,128)(2,1)} %get-tuple-element.12.q_ref, f32[2,16,128,128]{3,2,1,0:T(8,128)} %get-tuple-element.13.p_ref, f32[512,128]{1,0:T(8,128)} %get-tuple-element.14.ec_ref), custom_call_target="tpu_custom_call" | custom-call | tf_op jit(solution)/shard_map/finish/pallas_call | solution.py:410
  79.1 0.0 copy-done
  79.1 0.7 copy.17.gain_ref
  79.8 8.5 %decode.1 = (f32[64,2,16,128]{3,2,1,0:T(8,128)}, f32[40,256]{1,0:T(8,128)}) custom-call(s32[8]{0:T(128)} %slot_ref.1, f32[64,2,16,128]{3,2,1,0:T(8,128)} %bitcast.21, f32[8,2,16,128]{3,2,1,0:T(8,128)} %get-tuple-element.15.hand_ref, bf16[64,4,2,128]{3,2,1,0:T(2,128)(2,1)} %q_ref.1, bf16[64,4,2,128]{3,2,1,0:T(2,128)(2,1)} %k_ref.1, ...), custom_call_target="tpu_custom_call" | custom-call | tf_op jit(solution)/shard_map/decode/pallas_call | solution.py:473
  88.2 30.0 %project.1 = f32[2,6144]{1,0:T(2,128)} custom-call(f32[40,256]{1,0:T(8,128)} %get-tuple-element.17.z_ref, bf16[256,768]{1,0:T(8,128)(2,1)} %get-tuple-element.18.w_ref), custom_call_target="tpu_custom_call" | custom-call | tf_op jit(solution)/shard_map/project/pallas_call | solution.py:598
  118.3 1.4 %copy.19 = f32[2,6144]{1,0:T(2,128)} copy(f32[2,6144]{1,0:T(2,128)} %project.1) | data formatting | bytes 98304
Async XLA Ops:
  66.3 12.8 %copy-start = (f32[2,16]{1,0:T(2,128)S(1)}, f32[2,16]{1,0:T(2,128)}, u32[]{:S(2)}) copy-start(f32[2,16]{1,0:T(2,128)} %param.26) | copy-start | bytes 388

commit v2 on v1

--- a/solution.py
+++ b/solution.py
@@ -15,7 +15,8 @@
 T = 512
 CH = 128
 ROWS = 136
-FIRST_HEADS = 16
+FIRST_HEADS = 28
+UNROLL = 4
 
 
 def dot(a, b):
@@ -40,7 +41,7 @@
 def prefill_kernel(
     q_hbm, k_hbm, v_hbm, dec_ref, start_ref, w_ref,
     att_hbm, qh_hbm, p_ref, hand_ref, wt_ref, ec_ref,
-    raw, stage, qh, kt, vh, cum2, cum, s_ref, xbuf, tbuf, rbuf, pbuf, qbuf, obuf, pcur, fbuf, hbuf, wf, wr, abuf,
+    raw, qh, kt, vh, cum2, cum, s_ref, xbuf, tbuf, rbuf, pbuf, qbuf, obuf, pcur, fbuf, hbuf, wf, wr, att,
     load_sem, q_sem, att_sem, sa, ra, s1, r1, s2, r2, sb, rb, sh, rh, sw, rw,
 ):
     c, g = lax.axis_index("ctx"), lax.axis_index("grp")
@@ -51,14 +52,18 @@
     def peer(j):
         return (2 * j + core, g)
 
-    def load(which, hbm, at):
-        return pltpu.make_async_copy(
-            hbm.at[pl.ds(at * CH, CH)], raw.at[which, pl.ds(at * CH, CH)], load_sem.at[which, at]
-        )
-
-    for which, hbm in ((0, k_hbm), (1, v_hbm), (2, q_hbm)):
-        for at in range(T // CH):
-            load(which, hbm, at).start()
+    x, own_row = lax.rem(chip, 4), lax.div(chip, 4)
+    rows = (1 - own_row, own_row)
+
+    def load(which, hbm, row):
+        heads = pl.ds(pl.multiple_of(16 * row, 16), 16)
+        return pltpu.make_async_copy(hbm.at[:, heads], raw.at[which, row], load_sem.at[which, row])
+
+    for row in rows:
+        load(0, k_hbm, row).start()
+        load(1, v_hbm, row).start()
+    for row in rows:
+        load(2, q_hbm, row).start()
 
     bar = pltpu.get_barrier_semaphore()
     pl.semaphore_signal(bar, inc=1, device_id=partner, device_id_type=MESH)
@@ -71,36 +76,31 @@
     lax.fori_loop(1, 8, greet, 0)
 
     lane = lax.broadcasted_iota(jnp.int32, (H, T), 1)
-    x = dec_ref[...]
+    total = dec_ref[...]
     step = 1
     while step < T:
-        x = x + jnp.where(lane >= step, pltpu.roll(x, step, 1), 0.0)
+        total = total + jnp.where(lane >= step, pltpu.roll(total, step, 1), 0.0)
         step *= 2
-    cum[...] = x
-    cum2[...] = x * LOG2E
-    ec_ref[...] = jnp.concatenate([jnp.exp(x), jnp.zeros((HS - H, T), F32)], axis=0).T
-
-    def relay(which, hbm, at, put):
-        load(which, hbm, at).wait()
-        stage[...] = raw[which, pl.ds(at * CH, CH)].astype(F32).reshape(CH * H, HS)
-        for h in range(H):
-            put(h, pl.ds(pl.multiple_of(at * CH, CH), CH), stage[pl.ds(h, CH, stride=H), :])
-
-    def put_k(h, span, block):
-        kt[h, :, span] = block.T.astype(BF16)
-
-    def put_v(h, span, block):
-        vh[h, span, :] = block.astype(BF16)
-
-    def put_q(h, span, block):
-        qh[h, span, :] = block.astype(BF16)
-
-    def relay_kv(at, _):
-        relay(0, k_hbm, at, put_k)
-        relay(1, v_hbm, at, put_v)
-        return 0
-
-    lax.fori_loop(0, T // CH, relay_kv, 0)
+    cum[...] = total
+    cum2[...] = total * LOG2E
+    ec_ref[...] = jnp.concatenate([jnp.exp(total), jnp.zeros((HS - H, T), F32)], axis=0).T
+
+    def heads_first(which, row, at):
+        return jnp.swapaxes(raw[which, row, pl.ds(at * CH, CH)], 0, 1)
+
+    def relay_kv(row):
+        load(0, k_hbm, row).wait()
+        load(1, v_hbm, row).wait()
+
+        def chunk(at, _):
+            span = pl.ds(pl.multiple_of(at * CH, CH), CH)
+            vh[pl.ds(16 * row, 16), span, :] = heads_first(1, row, at)
+            block = heads_first(0, row, at)
+            for h in range(16):
+                kt[16 * row + h, :, span] = block[h].T
+            return 0
+
+        lax.fori_loop(0, T // CH, chunk, 0)
 
     def local_state(half, i):
         h = head_of(half, i)
@@ -111,33 +111,19 @@
         s_ref[half, i, 0:HS, :] = both[:HS] + both[HS:]
         s_ref[half, i, HS:ROWS, :] = jnp.broadcast_to(end, (ROWS - HS, HS))
 
-    def copy_a(m):
-        return remote(s_ref.at[other, pl.ds(4 * m, 4)], xbuf.at[pl.ds(4 * m, 4)], sa.at[m], ra.at[m], partner)
-
-    pl.semaphore_wait(bar, 15)
-
-    def other_half(m, _):
-        def one(i, _):
-            local_state(other, 4 * m + i)
-            return 0
-
-        lax.fori_loop(0, 4, one, 0)
-        copy_a(m).start()
-        return 0
-
-    lax.fori_loop(0, 4, other_half, 0)
-
-    def own_half(i, _):
-        local_state(core, i)
-        return 0
-
-    lax.fori_loop(0, 16, own_half, 0)
-
-    def wait_a(m, _):
-        copy_a(m).wait_recv()
-        return 0
-
-    lax.fori_loop(0, 4, wait_a, 0)
+    def copy_a(row):
+        part = pl.ds(8 * row, 8)
+        return remote(s_ref.at[other, part], xbuf.at[part], sa.at[row], ra.at[row], partner)
+
+    for row in rows:
+        relay_kv(row)
+        for i in range(8):
+            local_state(other, 8 * row + i)
+        if row is rows[0]:
+            pl.semaphore_wait(bar, 15)
+        copy_a(row).start()
+        for i in range(8):
+            local_state(core, 8 * row + i)
 
     def copy_1(j):
         return remote(tbuf.at[j], rbuf.at[chip], s1.at[j], r1.at[chip], peer(j))
@@ -155,13 +141,19 @@
             tbuf[j, r, 0:HS, :] = on_mine * mine[:HS] + on_theirs * theirs[:HS]
             tbuf[j, r, HS:ROWS, :] = mine[HS:] + theirs[HS:]
 
-    def send_total(d, _):
-        j = lax.rem(chip + d, 8)
-        chip_total(j)
-        copy_1(j).start()
-        return 0
-
-    lax.fori_loop(1, 8, send_total, 0)
+    def send_total(row):
+        def one(d, _):
+            j = 4 * row + lax.rem(x + d, 4)
+            chip_total(j)
+            copy_1(j).start()
+            return 0
+
+        return one
+
+    copy_a(rows[0]).wait_recv()
+    lax.fori_loop(0, 4, send_total(rows[0]), 0)
+    copy_a(rows[1]).wait_recv()
+    lax.fori_loop(1, 4, send_total(rows[1]), 0)
     chip_total(chip)
     rbuf[chip] = tbuf[chip]
 
@@ -181,20 +173,25 @@
     lax.fori_loop(1, 8, send_w, 0)
     wr[g] = wf[g]
 
-    def relay_q(at, _):
-        relay(2, q_hbm, at, put_q)
-        return 0
-
-    lax.fori_loop(0, T // CH, relay_q, 0)
+    for row in rows:
+        load(2, q_hbm, row).wait()
+
+        def relay_q(at, _):
+            span = pl.ds(pl.multiple_of(at * CH, CH), CH)
+            qh[pl.ds(16 * row, 16), span, :] = heads_first(2, row, at)
+            return 0
+
+        lax.fori_loop(0, T // CH, relay_q, 0)
     qh_copy = pltpu.make_async_copy(qh, qh_hbm, q_sem)
     qh_copy.start()
 
     causal = lax.broadcasted_iota(jnp.int32, (HS, HS), 0) >= lax.broadcasted_iota(jnp.int32, (HS, HS), 1)
 
-    def att_copy(h, slot):
-        return pltpu.make_async_copy(abuf.at[slot], att_hbm.at[h], att_sem.at[slot])
-
-    def attend(h, slot):
+    def att_copy(n):
+        part = pl.ds(UNROLL * n, UNROLL)
+        return pltpu.make_async_copy(att.at[part], att_hbm.at[part], att_sem.at[n])
+
+    def attend(h):
         row = cum2[pl.ds(h, 1), :]
         col = jnp.broadcast_to(row, (HS, T)).T
         left = dot(qh[h], kt[h, :, 0:256])
@@ -219,21 +216,16 @@
             jnp.concatenate([weigh(2, 0), weigh(2, 1), weigh(2, 2), none], axis=1),
             jnp.concatenate([weigh(3, 0), weigh(3, 1), weigh(3, 2), weigh(3, 3)], axis=1),
         ], axis=0)
-        abuf[slot, 0:256, :] = dot(top, v[0:256])
-        abuf[slot, 256:512, :] = dot(low, v)
-
-    def pair(n, _):
-        for slot in range(2):
-
-            @pl.when(n > 0)
-            def _():
-                att_copy(2 * n - 2 + slot, slot).wait()
-
-            attend(2 * n + slot, slot)
-            att_copy(2 * n + slot, slot).start()
-        return 0
-
-    lax.fori_loop(0, FIRST_HEADS // 2, pair, 0)
+        att[h, 0:256, :] = dot(top, v[0:256])
+        att[h, 256:512, :] = dot(low, v)
+
+    def some(n, _):
+        for u in range(UNROLL):
+            attend(UNROLL * n + u)
+        att_copy(n).start()
+        return 0
+
+    lax.fori_loop(0, FIRST_HEADS // UNROLL, some, 0)
 
     def copy_2(j):
         return remote(pbuf.at[j], qbuf.at[chip], s2.at[j], r2.at[chip], peer(j))
@@ -274,7 +266,7 @@
     lax.fori_loop(1, 8, send_h, 0)
     hbuf[g] = fbuf[g]
 
-    lax.fori_loop(FIRST_HEADS // 2, H // 2, pair, 0)
+    lax.fori_loop(FIRST_HEADS // UNROLL, H // UNROLL, some, 0)
 
     def copy_b(m):
         return remote(obuf.at[pl.ds(4 * m, 4)], p_ref.at[core, pl.ds(4 * m, 4)], sb.at[m], rb.at[m], partner)
@@ -313,17 +305,18 @@
         wt_ref[frm * 32 : (frm + 1) * 32, :] = wr[frm].astype(BF16)
     hand_ref[...] = hbuf[...]
 
-    for slot in range(2):
-        att_copy(H - 2 + slot, slot).wait()
+    for n in range(H // UNROLL):
+        att_copy(n).wait()
     qh_copy.wait()
 
     def finish_pair(m, _):
         arrival_b(m).wait_recv()
         copy_b(m).wait_send()
-        copy_a(m).wait_send()
         return 0
 
     lax.fori_loop(0, 4, finish_pair, 0)
+    for row in rows:
+        copy_a(row).wait_send()
 
     def finish(d, _):
         j = lax.rem(chip + d, 8)
@@ -355,8 +348,7 @@
         in_specs=[anywhere, anywhere, anywhere, vmem, vmem, vmem],
         out_specs=(anywhere, anywhere, vmem, vmem, vmem, vmem),
         scratch_shapes=[
-            pltpu.VMEM((3, T, H, HS), BF16),
-            pltpu.VMEM((CH * H, HS), F32),
+            pltpu.VMEM((3, 2, T, 16, HS), BF16),
             pltpu.VMEM((H, T, HS), BF16),
             pltpu.VMEM((H, HS, T), BF16),
             pltpu.VMEM((H, T, HS), BF16),
@@ -374,9 +366,9 @@
             pltpu.VMEM((8, 2, 16, HS), F32),
             pltpu.VMEM((8, 32, 768), F32),
             pltpu.VMEM((8, 32, 768), F32),
-            pltpu.VMEM((2, T, HS), F32),
-            dma((3, T // CH)), dma, dma((2,)),
-            dma((4,)), dma((4,)), dma((8,)), dma((8,)), dma((8,)), dma((8,)),
+            pltpu.VMEM((H, T, HS), F32),
+            dma((3, 2)), dma, dma((H // UNROLL,)),
+            dma((2,)), dma((2,)), dma((8,)), dma((8,)), dma((8,)), dma((8,)),
             dma((4,)), dma((4,)), dma((8,)), dma((8,)), dma((8,)), dma((8,)),
         ],
         compiler_params=pltpu.CompilerParams(
@@ -385,7 +377,7 @@
     )(q, k, v, decay, start, weight)
 
 
-def finish_kernel(att_ref, q_ref, p_ref, ec_ref, out_ref, wide, field, stage):
+def finish_kernel(att_ref, q_ref, p_ref, ec_ref, out_ref, wide, field):
     @pl.when(pl.program_id(0) == 0)
     def _():
         for h in range(H):
@@ -401,9 +393,7 @@
         squares = squares + x * x
     mean = jnp.sum(squares, axis=1, keepdims=True) / (H * HS)
     scale = jnp.broadcast_to(lax.rsqrt(mean + 1e-06), (CH, HS))
-    for h in range(H):
-        stage[pl.ds(h, CH, stride=H), :] = field[h] * scale
-    out_ref[...] = stage[...].reshape(CH, H, HS).astype(BF16)
+    out_ref[...] = jnp.swapaxes((field[...] * scale[None]).astype(BF16), 0, 1)
 
 
 def finish(att, qh, states, ec):
@@ -422,7 +412,6 @@
         scratch_shapes=[
             pltpu.VMEM((H, HS, 2 * HS), BF16),
             pltpu.VMEM((H, CH, HS), F32),
-            pltpu.VMEM((CH * H, HS), F32),
         ],
         compiler_params=pltpu.CompilerParams(vmem_limit_bytes=VMEM_LIMIT),
     )(att, qh, states, ec)
@@ -484,8 +473,14 @@
     )(slot, cache, hand, q, k, v, gate, decay, gain)
 
 
-def project_kernel(z_ref, w_ref, out_ref, zbuf, part, take, done, last, s1, r1, s2, r2, s3, r3):
+def project_kernel(z_ref, w_ref, out_ref, zbuf, part, half, take, done, last, s1, r1, sa, ra, s2, r2, s3, r3):
     c, g = lax.axis_index("ctx"), lax.axis_index("grp")
+    core, chip = lax.rem(c, 2), lax.div(c, 2)
+    partner = (2 * chip + 1 - core, g)
+
+    def peer(j):
+        return (2 * j + core, g)
+
     bar = pltpu.get_barrier_semaphore()
 
     def greet_grp(d, _):
@@ -493,12 +488,13 @@
         return 0
 
     def greet_ctx(d, _):
-        pl.semaphore_signal(bar, inc=1, device_id=(lax.rem(c + d, 16), g), device_id_type=MESH)
+        pl.semaphore_signal(bar, inc=1, device_id=peer(lax.rem(chip + d, 8)), device_id_type=MESH)
         return 0
 
     lax.fori_loop(1, 8, greet_grp, 0)
-    lax.fori_loop(1, 16, greet_ctx, 0)
-    pl.semaphore_wait(bar, 22)
+    lax.fori_loop(1, 8, greet_ctx, 0)
+    pl.semaphore_signal(bar, inc=1, device_id=partner, device_id_type=MESH)
+    pl.semaphore_wait(bar, 15)
 
     def copy_1(to):
         return remote(z_ref, zbuf.at[g], s1.at[to], r1.at[g], (c, to))
@@ -528,29 +524,38 @@
     for n in range(3):
         span = slice(n * 256, (n + 1) * 256)
         w = w_ref[:, span]
-        part[:, :, span] = (dot(hi, w) + dot(lo, w)).reshape(16, 16, 256)
-    part[:, :, 768:896] = squares.reshape(16, 16, HS)
+        both = (dot(hi, w) + dot(lo, w)).reshape(8, 2, 16, 256)
+        for k in range(2):
+            part[k, :, :, span] = both[:, k]
+    both = squares.reshape(8, 2, 16, HS)
+    for k in range(2):
+        part[k, :, :, 768:896] = both[:, k]
+
+    copy_a = remote(part.at[1 - core], half, sa, ra, partner)
+    copy_a.start()
+    copy_a.wait_recv()
+    half[...] = half[...] + part[core]
 
     def copy_2(to):
-        return remote(part.at[to], take.at[c], s2.at[to], r2.at[c], (to, g))
+        return remote(half.at[to], take.at[chip], s2.at[to], r2.at[chip], peer(to))
 
     def arrival_2(frm):
-        return remote(part.at[frm], take.at[frm], s2.at[frm], r2.at[frm], (frm, g))
+        return remote(half.at[frm], take.at[frm], s2.at[frm], r2.at[frm], peer(frm))
 
     def send_2(d, _):
-        copy_2(lax.rem(c + d, 16)).start()
-        return 0
-
-    lax.fori_loop(1, 16, send_2, 0)
-    take[c] = part[c]
+        copy_2(lax.rem(chip + d, 8)).start()
+        return 0
+
+    lax.fori_loop(1, 8, send_2, 0)
+    take[chip] = half[chip]
 
     def wait_2(d, _):
-        arrival_2(lax.rem(c + d, 16)).wait_recv()
-        return 0
-
-    lax.fori_loop(1, 16, wait_2, 0)
+        arrival_2(lax.rem(chip + d, 8)).wait_recv()
+        return 0
+
+    lax.fori_loop(1, 8, wait_2, 0)
     total = take[0]
-    for n in range(1, 16):
+    for n in range(1, 8):
         total = total + take[n]
     scale = lax.rsqrt(total[:, 768:769] / (H * HS) + 1e-06)
     total = total[:, :768] * scale
@@ -585,11 +590,12 @@
         return 0
 
     def end_ctx(d, _):
-        copy_2(lax.rem(c + d, 16)).wait_send()
+        copy_2(lax.rem(chip + d, 8)).wait_send()
         return 0
 
     lax.fori_loop(1, 8, end_grp, 0)
-    lax.fori_loop(1, 16, end_ctx, 0)
+    lax.fori_loop(1, 8, end_ctx, 0)
+    copy_a.wait_send()
 
 
 def project(z, weight):
@@ -603,11 +609,12 @@
         out_specs=vmem,
         scratch_shapes=[
             pltpu.VMEM((8, 40, 256), F32),
-            pltpu.VMEM((16, 16, 896), F32),
-            pltpu.VMEM((16, 16, 896), F32),
+            pltpu.VMEM((2, 8, 16, 896), F32),
+            pltpu.VMEM((8, 16, 896), F32),
+            pltpu.VMEM((8, 16, 896), F32),
             pltpu.VMEM((8, 2, 768), F32),
             pltpu.VMEM((8, 2, 768), F32),
-            dma((8,)), dma((8,)), dma((16,)), dma((16,)), dma((8,)), dma((8,)),
+            dma((8,)), dma((8,)), dma, dma, dma((8,)), dma((8,)), dma((8,)), dma((8,)),
         ],
         compiler_params=pltpu.CompilerParams(
             collective_id=1, has_side_effects=True, vmem_limit_bytes=VMEM_LIMIT

time: 121 us -> 100 us (0.83)
  Pallas kernels: 117 us -> 97 us
    pallas_call x1, Pallas kernels: 65.6 us -> 51.1 us  [prefill(): pl.pallas_call(prefill_kernel, name='prefill', out_shape=(jax.ShapeDtypeS...]
    pallas_call x1, Pallas kernels: 30 us -> 26.8 us  [project(): pl.pallas_call(project_kernel, name='project', out_shape=jax.ShapeDtypeSt...]
    pallas_call x1, Pallas kernels: 12.8 us -> 10.6 us  [finish(): pl.pallas_call(finish_kernel, name='finish', grid=(T // CH,), out_shape=j...]
where the time goes in v2:
time: 100 us; the launch traced here: 99.8 us
  Pallas kernels  97 us (97%)
  local copies, waits for them, and re-layouts  2.12 us (2%)
    pallas_call x1, Pallas kernels, prefill(): pl.pallas_call(prefill_kernel, name='prefill', out_shape=(jax.ShapeDtypeS...  51.1 us
    pallas_call x1, Pallas kernels, project(): pl.pallas_call(project_kernel, name='project', out_shape=jax.ShapeDtypeSt...  26.8 us
    pallas_call x1, Pallas kernels, finish(): pl.pallas_call(finish_kernel, name='finish', grid=(T // CH,), out_shape=j...  10.6 us
    pallas_call x1, Pallas kernels, decode(): pl.pallas_call(decode_kernel, name='decode', out_shape=(jax.ShapeDtypeStr...  8.48 us

profile of v2, /device:TPU:0, one launch (start us, length us, event | category | flops | bytes accessed | tf_op | source)
XLA Modules:
  0.0 99.8 jit_solution(16051444350690325433)
XLA Ops:
  0.6 51.1 %prefill.1 = (f32[32,512,128]{2,1,0:T(8,128)}, bf16[32,512,128]{2,1,0:T(8,128)(2,1)}, f32[2,16,128,128]{3,2,1,0:T(8,128)}, f32[8,2,16,128]{3,2,1,0:T(8,128)}, bf...) custom-call(bf16[512,32,128]{2,1,0:T(8,128)(2,1)} %bitcast.17, bf16[512,32,128]{2,1,0:T(8,128)(2,1)} %bitcast.18, ...), custom_call_target="tpu_custom_call" | custom-call | tf_op jit(solution)/shard_map/prefill/pallas_call | solution.py:337
  51.8 0.0 copy-start
  51.8 10.6 %finish.1 = bf16[512,32,128]{2,1,0:T(8,128)(2,1)} custom-call(f32[32,512,128]{2,1,0:T(8,128)} %get-tuple-element.11.att_ref, bf16[32,512,128]{2,1,0:T(8,128)(2,1)} %get-tuple-element.12.q_ref, f32[2,16,128,128]{3,2,1,0:T(8,128)} %get-tuple-element.13.p_ref, f32[512,128]{1,0:T(8,128)} %get-tuple-element.14.ec_ref), custom_call_target="tpu_custom_call" | custom-call | tf_op jit(solution)/shard_map/finish/pallas_call | solution.py:400
  62.4 0.0 copy-done
  62.4 0.7 copy.17.gain_ref
  63.1 8.5 %decode.1 = (f32[64,2,16,128]{3,2,1,0:T(8,128)}, f32[40,256]{1,0:T(8,128)}) custom-call(s32[8]{0:T(128)} %slot_ref.1, f32[64,2,16,128]{3,2,1,0:T(8,128)} %bitcast.21, f32[8,2,16,128]{3,2,1,0:T(8,128)} %get-tuple-element.15.hand_ref, bf16[64,4,2,128]{3,2,1,0:T(2,128)(2,1)} %q_ref.1, bf16[64,4,2,128]{3,2,1,0:T(2,128)(2,1)} %k_ref.1, ...), custom_call_target="tpu_custom_call" | custom-call | tf_op jit(solution)/shard_map/decode/pallas_call | solution.py:462
  71.6 26.8 %project.1 = f32[2,6144]{1,0:T(2,128)} custom-call(f32[40,256]{1,0:T(8,128)} %get-tuple-element.17.z_ref, bf16[256,768]{1,0:T(8,128)(2,1)} %get-tuple-element.18.w_ref), custom_call_target="tpu_custom_call" | custom-call | tf_op jit(solution)/shard_map/project/pallas_call | solution.py:604
  98.3 1.4 %copy.19 = f32[2,6144]{1,0:T(2,128)} copy(f32[2,6144]{1,0:T(2,128)} %project.1) | data formatting | bytes 98304
Async XLA Ops:
  51.8 10.6 %copy-start = (f32[2,16]{1,0:T(2,128)S(1)}, f32[2,16]{1,0:T(2,128)}, u32[]{:S(2)}) copy-start(f32[2,16]{1,0:T(2,128)} %param.26) | copy-start | bytes 388

commit v3 on v2

v3 whole, which is shorter than its diff:
```python
import jax
import jax.numpy as jnp
from jax import lax
from jax.experimental import pallas as pl
from jax.experimental.pallas import tpu as pltpu
from jax.sharding import PartitionSpec as P

H = 32
HS = 128
LOG2E = 1.4426950408889634
MESH = pl.DeviceIdType.MESH
F32 = jnp.float32
BF16 = jnp.bfloat16
VMEM_LIMIT = 60 * 1024 * 1024
T = 512
CH = 128
ROWS = 136
HEADS_AT_SCAN = 12
HEADS_AT_HAND = 24
UNROLL = 4


def dot(a, b):
    return lax.dot_general(a, b, (((1,), (0,)), ((), ())), preferred_element_type=F32)


def split(x):
    hi = x.astype(BF16)
    return hi, (x - hi.astype(F32)).astype(BF16)


def head_of(half, i):
    return 4 * lax.div(i, 2) + 2 * half + lax.rem(i, 2)


def remote(src, dst, send, recv, where):
    return pltpu.make_async_remote_copy(
        src_ref=src, dst_ref=dst, send_sem=send, recv_sem=recv, device_id=where, device_id_type=MESH
    )


def kernel(
    slot_ref, q_hbm, k_hbm, v_hbm, dec_ref, start_ref, w_ref, cache_hbm, dq_ref, dk_ref, dv_ref, gate_ref, decay_ref, gain_ref,
    out_hbm, new_hbm, decoded_ref,
    raw, qh, kt, vh, cum2, cum, ec, s_ref, xbuf, tbuf, rbuf, pbuf, qbuf, obuf, states, pcur, fbuf, hbuf, wf, wr, wt, att,
    wide, outs, cache, merged, zrow, zmine, zbuf, part, half, take, done, last,
    load_sem, cache_sem, new_sem, out_sem, sa, ra, s1, r1, s2, r2, sb, rb, sh, rh, sw, rw, sz, rz, sc, rc, sp, rp, sd, rd,
):
    c, g = lax.axis_index("ctx"), lax.axis_index("grp")
    core, chip = lax.rem(c, 2), lax.div(c, 2)
    other = 1 - core
    partner = (2 * chip + other, g)

    def peer(j):
        return (2 * j + core, g)

    x, own_row = lax.rem(chip, 4), lax.div(chip, 4)
    rows = (1 - own_row, own_row)

    def load(which, hbm, row):
        heads = pl.ds(pl.multiple_of(16 * row, 16), 16)
        return pltpu.make_async_copy(hbm.at[:, heads], raw.at[which, row], load_sem.at[which, row])

    for row in rows:
        load(0, k_hbm, row).start()
        load(1, v_hbm, row).start()
    for row in rows:
        load(2, q_hbm, row).start()
    cache_load = pltpu.make_async_copy(cache_hbm, cache.at[pl.ds(0, 64)], cache_sem)
    cache_load.start()

    bar = pltpu.get_barrier_semaphore()
    pl.semaphore_signal(bar, inc=1, device_id=partner, device_id_type=MESH)

    def greet(d, _):
        pl.semaphore_signal(bar, inc=1, device_id=peer(lax.rem(chip + d, 8)), device_id_type=MESH)
        pl.semaphore_signal(bar, inc=1, device_id=(c, lax.rem(g + d, 8)), device_id_type=MESH)
        return 0

    lax.fori_loop(1, 8, greet, 0)

    lane = lax.broadcasted_iota(jnp.int32, (H, T), 1)
    total = dec_ref[...]
    step = 1
    while step < T:
        total = total + jnp.where(lane >= step, pltpu.roll(total, step, 1), 0.0)
        step *= 2
    cum[...] = total
    cum2[...] = total * LOG2E
    ec[...] = jnp.concatenate([jnp.exp(total), jnp.zeros((HS - H, T), F32)], axis=0).T

    def heads_first(which, row, at):
        return jnp.swapaxes(raw[which, row, pl.ds(at * CH, CH)], 0, 1)

    def relay_kv(row):
        load(0, k_hbm, row).wait()
        load(1, v_hbm, row).wait()

        def chunk(at, _):
            span = pl.ds(pl.multiple_of(at * CH, CH), CH)
            vh[pl.ds(16 * row, 16), span, :] = heads_first(1, row, at)
            block = heads_first(0, row, at)
            for h in range(16):
                kt[16 * row + h, :, span] = block[h].T
            return 0

        lax.fori_loop(0, T // CH, chunk, 0)

    def local_state(half, i):
        h = head_of(half, i)
        row = cum[pl.ds(h, 1), :]
        end = row[:, T - 1 : T]
        hi, lo = split(kt[h].astype(F32) * jnp.exp(end - row))
        both = dot(jnp.concatenate([hi, lo], axis=0), vh[h])
        s_ref[half, i, 0:HS, :] = both[:HS] + both[HS:]
        s_ref[half, i, HS:ROWS, :] = jnp.broadcast_to(end, (ROWS - HS, HS))

    def copy_a(row):
        part = pl.ds(8 * row, 8)
        return remote(s_ref.at[other, part], xbuf.at[part], sa.at[row], ra.at[row], partner)

    for row in rows:
        relay_kv(row)
        for i in range(8):
            local_state(other, 8 * row + i)
        if row is rows[0]:
            pl.semaphore_wait(bar, 15)
        copy_a(row).start()
        for i in range(8):
            local_state(core, 8 * row + i)

    def copy_1(j):
        return remote(tbuf.at[j], rbuf.at[chip], s1.at[j], r1.at[chip], peer(j))

    def arrival_1(j):
        return remote(tbuf.at[j], rbuf.at[j], s1.at[j], r1.at[j], peer(j))

    def chip_total(j):
        for r in range(2):
            i = 2 * j + r
            mine, theirs = s_ref[core, i], xbuf[i]
            end_mine, end_theirs = mine[HS : HS + 1], theirs[HS : HS + 1]
            on_mine = jnp.where(core == 0, jnp.exp(end_theirs), 1.0)
            on_theirs = jnp.where(core == 0, 1.0, jnp.exp(end_mine))
            tbuf[j, r, 0:HS, :] = on_mine * mine[:HS] + on_theirs * theirs[:HS]
            tbuf[j, r, HS:ROWS, :] = mine[HS:] + theirs[HS:]

    def send_total(row):
        def one(d, _):
            j = 4 * row + lax.rem(x + d, 4)
            chip_total(j)
            copy_1(j).start()
            return 0

        return one

    copy_a(rows[0]).wait_recv()
    lax.fori_loop(0, 4, send_total(rows[0]), 0)
    copy_a(rows[1]).wait_recv()
    lax.fori_loop(1, 4, send_total(rows[1]), 0)
    chip_total(chip)
    rbuf[chip] = tbuf[chip]

    for to in range(8):
        wf[to] = w_ref[:, to * 768 : (to + 1) * 768].astype(F32)

    def copy_w(to):
        return remote(wf.at[to], wr.at[g], sw.at[to], rw.at[g], (c, to))

    def arrival_w(frm):
        return remote(wf.at[frm], wr.at[frm], sw.at[frm], rw.at[frm], (c, frm))

    def send_w(d, _):
        copy_w(lax.rem(g + d, 8)).start()
        return 0

    lax.fori_loop(1, 8, send_w, 0)
    wr[g] = wf[g]

    for row in rows:
        load(2, q_hbm, row).wait()

        def relay_q(at, _):
            span = pl.ds(pl.multiple_of(at * CH, CH), CH)
            qh[pl.ds(16 * row, 16), span, :] = heads_first(2, row, at)
            return 0

        lax.fori_loop(0, T // CH, relay_q, 0)

    lane = lax.broadcasted_iota(jnp.int32, (16, 64), 1)
    pick = lax.broadcasted_iota(jnp.int32, (8, 64), 1)
    scale = jnp.exp(decay_ref[...])

    def decode_row(at, s, ys):
        here = lane == s
        q, k = dq_ref[s].astype(F32), dk_ref[s].astype(F32)
        factor = jnp.sum(jnp.where(pick == s, scale, 0.0), axis=1, keepdims=True)
        ys = list(ys)
        for h in range(2):
            state = cache[at, h]
            for i in range(4):
                value = jnp.sum(jnp.where(here, dv_ref[i, h].astype(F32), 0.0), axis=1, keepdims=True)
                state = factor[2 * i + h : 2 * i + h + 1] * state + value * k[i, h : h + 1, :]
                y = jnp.sum(state * q[i, h : h + 1, :], axis=1, keepdims=True)
                ys[2 * i + h] = jnp.where(here, y, ys[2 * i + h])
            cache[at, h] = state
        return tuple(ys)

    cache_load.wait()
    ys = lax.fori_loop(
        0, 64, lambda s, ys: decode_row(s, s, ys), tuple(jnp.zeros((16, 64), F32) for _ in range(8)), unroll=2
    )

    causal = lax.broadcasted_iota(jnp.int32, (HS, HS), 0) >= lax.broadcasted_iota(jnp.int32, (HS, HS), 1)

    def attend(h):
        row = cum2[pl.ds(h, 1), :]
        col = jnp.broadcast_to(row, (HS, T)).T
        left = dot(qh[h], kt[h, :, 0:256])
        right = dot(qh[h, 256:512, :], kt[h, :, 256:512])

        def weigh(a, b):
            scores = left if b < 2 else right
            first = a if b < 2 else a - 2
            part = scores[first * HS : (first + 1) * HS, (b % 2) * HS : (b % 2 + 1) * HS]
            diff = col[a * HS : (a + 1) * HS] - row[:, b * HS : (b + 1) * HS]
            if a == b:
                diff = jnp.where(causal, diff, -1e30)
            return (part * jnp.exp2(diff)).astype(BF16)

        v = vh[h]
        none = jnp.zeros((HS, HS), BF16)
        top = jnp.concatenate([
            jnp.concatenate([weigh(0, 0), none], axis=1),
            jnp.concatenate([weigh(1, 0), weigh(1, 1)], axis=1),
        ], axis=0)
        low = jnp.concatenate([
            jnp.concatenate([weigh(2, 0), weigh(2, 1), weigh(2, 2), none], axis=1),
            jnp.concatenate([weigh(3, 0), weigh(3, 1), weigh(3, 2), weigh(3, 3)], axis=1),
        ], axis=0)
        att[h, 0:256, :] = dot(top, v[0:256])
        att[h, 256:512, :] = dot(low, v)

    def some(n, _):
        for u in range(UNROLL):
            attend(UNROLL * n + u)
        return 0

    lax.fori_loop(0, HEADS_AT_SCAN // UNROLL, some, 0)

    def copy_2(j):
        return remote(pbuf.at[j], qbuf.at[chip], s2.at[j], r2.at[chip], peer(j))

    def arrival_2(j):
        return remote(pbuf.at[j], qbuf.at[j], s2.at[j], r2.at[j], peer(j))

    pcur[...] = start_ref[...]

    def scan(j, _):
        pbuf[j] = pcur[...]

        @pl.when(j != chip)
        def _():
            copy_2(j).start()
            arrival_1(j).wait_recv()

        for r in range(2):
            pcur[r] = jnp.exp(rbuf[j, r, HS : HS + 1, :]) * pcur[r] + rbuf[j, r, 0:HS, :]
        return 0

    lax.fori_loop(0, 8, scan, 0)
    qbuf[chip] = pbuf[chip]

    for r in range(2):
        fbuf[:, r] = pcur[r].T.reshape(8, 16, HS)

    def copy_h(to):
        return remote(fbuf.at[to], hbuf.at[g], sh.at[to], rh.at[g], (c, to))

    def arrival_h(frm):
        return remote(fbuf.at[frm], hbuf.at[frm], sh.at[frm], rh.at[frm], (c, frm))

    def send_h(d, _):
        copy_h(lax.rem(g + d, 8)).start()
        return 0

    lax.fori_loop(1, 8, send_h, 0)
    hbuf[g] = fbuf[g]

    lax.fori_loop(HEADS_AT_SCAN // UNROLL, HEADS_AT_HAND // UNROLL, some, 0)

    def take_h(d, _):
        frm = lax.rem(g + d, 8)
        arrival_h(frm).wait_recv()
        arrival_w(frm).wait_recv()
        return 0

    lax.fori_loop(1, 8, take_h, 0)
    cache[64:72] = hbuf[...]
    ys = lax.fori_loop(0, 8, lambda p, ys: decode_row(64 + p, slot_ref[p], ys), ys, unroll=2)
    for i in range(4):
        squares = jnp.zeros((1, 64), F32)
        parts = []
        for h in range(2):
            y = ys[2 * i + h]
            squares = squares + jnp.sum(y * y, axis=0, keepdims=True)
            parts.append(y * gain_ref[h] * jax.nn.sigmoid(gate_ref[i, h].astype(F32)))
        parts.append(jnp.broadcast_to(squares, (8, 64)))
        parts.append(jnp.zeros((HS - 40, 64), F32))
        zrow[pl.ds(i, 64, stride=4), :] = jnp.concatenate(parts, axis=0).T
    zmine[...] = zrow[...].T[:40]

    def copy_z(to):
        return remote(zmine, zbuf.at[g], sz.at[to], rz.at[g], (c, to))

    def arrival_z(frm):
        return remote(zmine, zbuf.at[frm], sz.at[frm], rz.at[frm], (c, frm))

    def send_z(d, _):
        copy_z(lax.rem(g + d, 8)).start()
        return 0

    lax.fori_loop(1, 8, send_z, 0)
    zbuf[g] = zmine[...]

    for frm in range(8):
        wt[frm * 32 : (frm + 1) * 32, :] = wr[frm].astype(BF16)
    lax.fori_loop(HEADS_AT_HAND // UNROLL, H // UNROLL, some, 0)

    def wait_z(d, _):
        arrival_z(lax.rem(g + d, 8)).wait_recv()
        return 0

    lax.fori_loop(1, 8, wait_z, 0)
    z = jnp.concatenate([zbuf[n, 0:32, :] for n in range(8)], axis=0).T
    squares = zbuf[0, 32:40, :]
    for n in range(1, 8):
        squares = squares + zbuf[n, 32:40, :]
    squares = jnp.concatenate([squares] * 16, axis=0).T
    hi, lo = split(z)
    for n in range(3):
        span = slice(n * 256, (n + 1) * 256)
        w = wt[:, span]
        both = (dot(hi, w) + dot(lo, w)).reshape(8, 2, 16, 256)
        for k in range(2):
            part[k, :, :, span] = both[:, k]
    both = squares.reshape(8, 2, 16, HS)
    for k in range(2):
        part[k, :, :, 768:896] = both[:, k]
    copy_c = remote(part.at[other], half, sc, rc, partner)
    copy_c.start()

    def copy_b(m):
        return remote(obuf.at[pl.ds(4 * m, 4)], states.at[core, pl.ds(4 * m, 4)], sb.at[m], rb.at[m], partner)

    def arrival_b(m):
        return remote(obuf.at[pl.ds(4 * m, 4)], states.at[other, pl.ds(4 * m, 4)], sb.at[m], rb.at[m], partner)

    def spread(m, _):
        for n in range(2):
            j = 2 * m + n

            @pl.when(j != chip)
            def _():
                arrival_2(j).wait_recv()

            for r in range(2):
                i = 2 * j + r
                before = qbuf[j, r]
                first = jnp.where(core == 0, s_ref[core, i], xbuf[i])
                after = jnp.exp(first[HS : HS + 1]) * before + first[:HS]
                states[core, i] = jnp.where(core == 0, before, after)
                obuf[i] = jnp.where(core == 0, after, before)
        copy_b(m).start()
        return 0

    lax.fori_loop(0, 4, spread, 0)

    copy_c.wait_recv()
    half[...] = half[...] + part[core]

    def copy_p(to):
        return remote(half.at[to], take.at[chip], sp.at[to], rp.at[chip], peer(to))

    def arrival_p(frm):
        return remote(half.at[frm], take.at[frm], sp.at[frm], rp.at[frm], peer(frm))

    def send_p(d, _):
        copy_p(lax.rem(chip + d, 8)).start()
        return 0

    lax.fori_loop(1, 8, send_p, 0)
    take[chip] = half[chip]

    def take_b(m, _):
        arrival_b(m).wait_recv()
        return 0

    lax.fori_loop(0, 4, take_b, 0)
    for h in range(H):
        hi, lo = split(states[(h // 2) % 2, 2 * (h // 4) + h % 2])
        wide[h, :, 0:HS] = hi
        wide[h, :, HS:] = lo

    def out_copy(at, slot):
        return pltpu.make_async_copy(outs.at[slot], out_hbm.at[pl.ds(at * CH, CH)], out_sem.at[slot])

    for at in range(T // CH):
        span = slice(at * CH, (at + 1) * CH)
        squares = jnp.zeros((CH, HS), F32)
        for h in range(H):
            both = dot(qh[h, span, :], wide[h])
            field = att[h, span, :] + (both[:, :HS] + both[:, HS:]) * ec[span, h : h + 1]
            att[h, span, :] = field
            squares = squares + field * field
        mean = jnp.sum(squares, axis=1, keepdims=True) / (H * HS)
        factor = jnp.broadcast_to(lax.rsqrt(mean + 1e-06), (CH, HS))
        if at >= 2:
            out_copy(at - 2, at % 2).wait()
        outs[at % 2] = jnp.swapaxes((att[:, span, :] * factor[None]).astype(BF16), 0, 1)
        out_copy(at, at % 2).start()

    def wait_p(d, _):
        arrival_p(lax.rem(chip + d, 8)).wait_recv()
        return 0

    lax.fori_loop(1, 8, wait_p, 0)
    total = take[0]
    for n in range(1, 8):
        total = total + take[n]
    total = total[:, :768] * lax.rsqrt(total[:, 768:769] / (H * HS) + 1e-06)
    for n in range(8):
        done[n] = total[2 * n : 2 * n + 2]

    def copy_d(to):
        return remote(done.at[to], last.at[g], sd.at[to], rd.at[g], (c, to))

    def arrival_d(frm):
        return remote(done.at[frm], last.at[frm], sd.at[frm], rd.at[frm], (c, frm))

    def send_d(d, _):
        copy_d(lax.rem(g + d, 8)).start()
        return 0

    lax.fori_loop(1, 8, send_d, 0)
    last[g] = done[g]

    def merge(s, _):
        at = s
        for p in range(8):
            at = jnp.where(slot_ref[p] == s, 64 + p, at)
        merged[s] = cache[at]
        return 0

    lax.fori_loop(0, 64, merge, 0)
    new_copy = pltpu.make_async_copy(merged, new_hbm, new_sem)
    new_copy.start()

    def wait_d(d, _):
        arrival_d(lax.rem(g + d, 8)).wait_recv()
        return 0

    lax.fori_loop(1, 8, wait_d, 0)
    for n in range(8):
        decoded_ref[:, n * 768 : (n + 1) * 768] = last[n]

    out_copy(2, 0).wait()
    out_copy(3, 1).wait()
    new_copy.wait()
    for row in rows:
        copy_a(row).wait_send()
    copy_c.wait_send()

    def finish_pair(m, _):
        copy_b(m).wait_send()
        return 0

    lax.fori_loop(0, 4, finish_pair, 0)

    def finish(d, _):
        j = lax.rem(chip + d, 8)
        copy_1(j).wait_send()
        copy_2(j).wait_send()
        copy_p(j).wait_send()
        to = lax.rem(g + d, 8)
        copy_w(to).wait_send()
        copy_h(to).wait_send()
        copy_z(to).wait_send()
        copy_d(to).wait_send()
        return 0

    lax.fori_loop(1, 8, finish, 0)


def per_device(
    queries, keys, values, prefill_decay, start_states, resident_states, slot_of_prompt,
    decode_queries, decode_keys, decode_values, decode_gate, decode_decay, norm_gain, out_weight,
):
    dma = pltpu.SemaphoreType.DMA
    hbm, vmem = pl.BlockSpec(memory_space=pl.ANY), pl.BlockSpec(memory_space=pltpu.VMEM)
    prefill_out, cache, decoded = pl.pallas_call(
        kernel,
        name="lightning",
        out_shape=(
            jax.ShapeDtypeStruct((T, H, HS), BF16),
            jax.ShapeDtypeStruct((64, 2, 16, HS), F32),
            jax.ShapeDtypeStruct((2, 6144), F32),
        ),
        in_specs=[pl.BlockSpec(memory_space=pltpu.SMEM), hbm, hbm, hbm, vmem, vmem, vmem, hbm] + [vmem] * 6,
        out_specs=(hbm, hbm, vmem),
        scratch_shapes=[
            pltpu.VMEM((3, 2, T, 16, HS), BF16),
            pltpu.VMEM((H, T, HS), BF16),
            pltpu.VMEM((H, HS, T), BF16),
            pltpu.VMEM((H, T, HS), BF16),
            pltpu.VMEM((H, T), F32),
            pltpu.VMEM((H, T), F32),
            pltpu.VMEM((T, HS), F32),
            pltpu.VMEM((2, 16, ROWS, HS), F32),
            pltpu.VMEM((16, ROWS, HS), F32),
            pltpu.VMEM((8, 2, ROWS, HS), F32),
            pltpu.VMEM((8, 2, ROWS, HS), F32),
            pltpu.VMEM((8, 2, HS, HS), F32),
            pltpu.VMEM((8, 2, HS, HS), F32),
            pltpu.VMEM((16, HS, HS), F32),
            pltpu.VMEM((2, 16, HS, HS), F32),
            pltpu.VMEM((2, HS, HS), F32),
            pltpu.VMEM((8, 2, 16, HS), F32),
            pltpu.VMEM((8, 2, 16, HS), F32),
            pltpu.VMEM((8, 32, 768), F32),
            pltpu.VMEM((8, 32, 768), F32),
            pltpu.VMEM((256, 768), BF16),
            pltpu.VMEM((H, T, HS), F32),
            pltpu.VMEM((H, HS, 2 * HS), BF16),
            pltpu.VMEM((2, CH, H, HS), BF16),
            pltpu.VMEM((72, 2, 16, HS), F32),
            pltpu.VMEM((64, 2, 16, HS), F32),
            pltpu.VMEM((256, HS), F32),
            pltpu.VMEM((40, 256), F32),
            pltpu.VMEM((8, 40, 256), F32),
            pltpu.VMEM((2, 8, 16, 896), F32),
            pltpu.VMEM((8, 16, 896), F32),
            pltpu.VMEM((8, 16, 896), F32),
            pltpu.VMEM((8, 2, 768), F32),
            pltpu.VMEM((8, 2, 768), F32),
            dma((3, 2)), dma, dma, dma((2,)),
            dma((2,)), dma((2,)), dma((8,)), dma((8,)), dma((8,)), dma((8,)),
            dma((4,)), dma((4,)), dma((8,)), dma((8,)), dma((8,)), dma((8,)),
            dma((8,)), dma((8,)), dma, dma, dma((8,)), dma((8,)), dma((8,)), dma((8,)),
        ],
        compiler_params=pltpu.CompilerParams(
            collective_id=0, has_side_effects=True, vmem_limit_bytes=VMEM_LIMIT
        ),
    )(
        slot_of_prompt,
        queries[0],
        keys[0],
        values[0],
        jnp.swapaxes(prefill_decay[0], 0, 1),
        start_states[0],
        out_weight.reshape(32, 6144),
        jnp.swapaxes(resident_states, 2, 3),
        decode_queries,
        decode_keys,
        jnp.transpose(decode_values, (1, 2, 3, 0)),
        jnp.transpose(decode_gate, (1, 2, 3, 0)),
        jnp.transpose(decode_decay, (1, 2, 0)).reshape(8, 64),
        norm_gain[:, :, None],
    )
    return prefill_out[None], jnp.swapaxes(cache, 2, 3), decoded


def solution(mesh):
    return jax.shard_map(
        per_device,
        mesh=mesh,
        in_specs=(
            P("grp", "ctx", None, None),
            P("grp", "ctx", None, None),
            P("grp", "ctx", None, None),
            P("grp", "ctx", None),
            P("grp", "ctx", None, None),
            P(None, "ctx", None, "grp"),
            P(),
            P(None, None, "ctx", None),
            P(None, None, "ctx", None),
            P(None, None, "ctx", "grp"),
            P(None, None, "ctx", "grp"),
            P(None, None, "ctx"),
            P("ctx", "grp"),
            P("ctx", "grp", None),
        ),
        out_specs=(
            P("grp", "ctx", None, None),
            P(None, "ctx", None, "grp"),
            P(("ctx", "grp"), None),
        ),
        check_vma=False,
    )
```

time: 100 us -> 82.3 us (0.82)
  Pallas kernels: 97 us -> 73 us
  local copies, waits for them, and re-layouts: 2.12 us -> 7.97 us
    pallas_call x4 -> x1, Pallas kernels: 97 us -> 73 us  [per_device(): pl.pallas_call(kernel, name='lightning', out_shape=(jax.ShapeDtypeStruct(...]
    unnamed x3 -> x7, local copies, waits for them, and re-layouts: 1.43 us -> 6.6 us
where the time goes in v3:
time: 82.3 us; the launch traced here: 81.6 us
  Pallas kernels  73 us (89%)
  local copies, waits for them, and re-layouts  7.97 us (10%)
    pallas_call x1, Pallas kernels, per_device(): pl.pallas_call(kernel, name='lightning', out_shape=(jax.ShapeDtypeStruct(...  73 us
    unnamed x7, local copies, waits for them, and re-layouts  6.6 us

profile of v3, /device:TPU:0, one launch (start us, length us, event | category | flops | bytes accessed | tf_op | source)
XLA Modules:
  0.0 81.6 jit_solution(14413960519992806651)
XLA Ops:
  0.6 1.4 %copy.17.gain_ref = f32[2,16,1]{2,1,0:T(8,128)} copy(f32[2,16,1]{1,0,2:T(2,128)} %bitcast.29) | data formatting | bytes 256 | tf_op jit(solution)/shard_map/broadcast_in_dim | solution.py:568
  2.0 73.0 %lightning.1 = (bf16[512,32,128]{2,1,0:T(8,128)(2,1)}, f32[64,2,16,128]{3,2,1,0:T(8,128)}, f32[2,6144]{1,0:T(2,128)}) custom-call(s32[8]{0:T(128)} %slot_ref.1, bf16[512,32,128]{2,1,0:T(8,128)(2,1)} %bitcast.18, bf16[512,32,128]{2,1,0:T(8,128)(2,1)} %bitcast.19, bf16[512,32,128]{2,1,0:T(8,128)(2,1)} %bitcast.20, f32[32,512]{1,0:T(8,128)} %bitcast.25, ...), custom_call_target="tpu_custom_call" | custom-call | tf_op jit(solution)/shard_map/lightning/pallas_call | solution.py:501
  75.0 0.0 copy-start
  75.0 0.0 copy-start.1
  75.0 5.0 %copy.21 = bf16[1,512,32,128]{3,2,1,0:T(8,128)(2,1)} copy(bf16[1,512,32,128]{3,2,1,0:T(8,128)(2,1)} %bitcast.17) | data formatting | bytes 8388608
  80.0 0.0 copy-done
  80.0 1.0 %copy.22 = f32[64,2,128,16]{2,3,1,0:T(8,128)} copy(f32[64,2,128,16]{2,3,1,0:T(8,128)S(1)} %bitcast.21) | data formatting | bytes 2097152
  81.0 0.0 copy-done.1
  81.0 0.6 copy.23
Async XLA Ops:
  75.0 5.0 %copy-start = (f32[64,2,16,128]{3,2,1,0:T(8,128)S(1)}, f32[64,2,16,128]{3,2,1,0:T(8,128)}, u32[]{:S(2)}) copy-start(f32[64,2,16,128]{3,2,1,0:T(8,128)} %get-tuple-element.7) | copy-start | bytes 3145732
  75.0 6.0 %copy-start.1 = (f32[2,6144]{1,0:T(2,128)S(1)}, f32[2,6144]{1,0:T(2,128)}, u32[]{:S(2)}) copy-start(f32[2,6144]{1,0:T(2,128)} %get-tuple-element.14) | copy-start | bytes 147460

commit v4 on v3

--- a/solution.py
+++ b/solution.py
@@ -15,8 +15,9 @@
 T = 512
 CH = 128
 ROWS = 136
-HEADS_AT_SCAN = 12
-HEADS_AT_HAND = 24
+HEADS_AT_SCAN = 8
+HEADS_AT_GATHER = 16
+HEADS_AT_SUM = 20
 UNROLL = 4
 
 
@@ -44,7 +45,8 @@
     out_hbm, new_hbm, decoded_ref,
     raw, qh, kt, vh, cum2, cum, ec, s_ref, xbuf, tbuf, rbuf, pbuf, qbuf, obuf, states, pcur, fbuf, hbuf, wf, wr, wt, att,
     wide, outs, cache, merged, zrow, zmine, zbuf, part, half, take, done, last,
-    load_sem, cache_sem, new_sem, out_sem, sa, ra, s1, r1, s2, r2, sb, rb, sh, rh, sw, rw, sz, rz, sc, rc, sp, rp, sd, rd,
+    gated, given, taken, ymine, ybuf, place,
+    load_sem, cache_sem, new_sem, out_sem, sa, ra, s1, r1, s2, r2, sb, rb, sh, rh, sw, rw, sz, rz, sc, rc, sp, rp, sd, rd, sv, rv, sy, ry,
 ):
     c, g = lax.axis_index("ctx"), lax.axis_index("grp")
     core, chip = lax.rem(c, 2), lax.div(c, 2)
@@ -119,16 +121,6 @@
         part = pl.ds(8 * row, 8)
         return remote(s_ref.at[other, part], xbuf.at[part], sa.at[row], ra.at[row], partner)
 
-    for row in rows:
-        relay_kv(row)
-        for i in range(8):
-            local_state(other, 8 * row + i)
-        if row is rows[0]:
-            pl.semaphore_wait(bar, 15)
-        copy_a(row).start()
-        for i in range(8):
-            local_state(core, 8 * row + i)
-
     def copy_1(j):
         return remote(tbuf.at[j], rbuf.at[chip], s1.at[j], r1.at[chip], peer(j))
 
@@ -154,29 +146,41 @@
 
         return one
 
+    def local_states(row):
+        for i in range(8):
+            local_state(other, 8 * row + i)
+        copy_a(row).start()
+        for i in range(8):
+            local_state(core, 8 * row + i)
+
+    pl.semaphore_wait(bar, 15)
+    for to in range(8):
+        wf[to] = w_ref[:, to * 768 : (to + 1) * 768].astype(F32)
+
+    def copy_w(to):
+        return remote(wf.at[to], wr.at[g], sw.at[to], rw.at[g], (c, to))
+
+    def arrival_w(frm):
+        return remote(wf.at[frm], wr.at[frm], sw.at[frm], rw.at[frm], (c, frm))
+
+    def send_w(d, _):
+        copy_w(lax.rem(g + d, 8)).start()
+        return 0
+
+    lax.fori_loop(1, 8, send_w, 0)
+    wr[g] = wf[g]
+
+    relay_kv(rows[0])
+    local_states(rows[0])
+    relay_kv(rows[1])
     copy_a(rows[0]).wait_recv()
     lax.fori_loop(0, 4, send_total(rows[0]), 0)
+    local_states(rows[1])
     copy_a(rows[1]).wait_recv()
     lax.fori_loop(1, 4, send_total(rows[1]), 0)
     chip_total(chip)
     rbuf[chip] = tbuf[chip]
 
-    for to in range(8):
-        wf[to] = w_ref[:, to * 768 : (to + 1) * 768].astype(F32)
-
-    def copy_w(to):
-        return remote(wf.at[to], wr.at[g], sw.at[to], rw.at[g], (c, to))
-
-    def arrival_w(frm):
-        return remote(wf.at[frm], wr.at[frm], sw.at[frm], rw.at[frm], (c, frm))
-
-    def send_w(d, _):
-        copy_w(lax.rem(g + d, 8)).start()
-        return 0
-
-    lax.fori_loop(1, 8, send_w, 0)
-    wr[g] = wf[g]
-
     for row in rows:
         load(2, q_hbm, row).wait()
 
@@ -188,6 +192,41 @@
         lax.fori_loop(0, T // CH, relay_q, 0)
 
     lane = lax.broadcasted_iota(jnp.int32, (16, 64), 1)
+    wide_lane = lax.broadcasted_iota(jnp.int32, (16, HS), 1)
+    diagonal = lax.broadcasted_iota(jnp.int32, (16, 16), 0) == lax.broadcasted_iota(jnp.int32, (16, 16), 1)
+    for h in range(2):
+        spread_gain = jnp.broadcast_to(gain_ref[h : h + 1, :], (16, 16))
+        gain = jnp.sum(jnp.where(diagonal, spread_gain, 0.0), axis=1, keepdims=True)
+        for i in range(4):
+            gated[i, h] = gain * jax.nn.sigmoid(gate_ref[i, h].astype(F32))
+
+    def give(p, _):
+        here = lane == slot_ref[p]
+        message = jnp.zeros((16, HS), F32)
+        for h in range(2):
+            for i in range(4):
+                value = jnp.sum(jnp.where(here, dv_ref[i, h].astype(F32), 0.0), axis=1, keepdims=True)
+                factor = jnp.sum(jnp.where(here, gated[i, h], 0.0), axis=1, keepdims=True)
+                message = jnp.where(wide_lane == 4 * h + i, value, message)
+                message = jnp.where(wide_lane == 8 + 4 * h + i, factor, message)
+        given[p] = message
+        return 0
+
+    lax.fori_loop(0, 8, give, 0)
+
+    def copy_v(to):
+        return remote(given.at[to], taken.at[g], sv.at[to], rv.at[g], (c, to))
+
+    def arrival_v(frm):
+        return remote(given.at[frm], taken.at[frm], sv.at[frm], rv.at[frm], (c, frm))
+
+    def send_v(d, _):
+        copy_v(lax.rem(g + d, 8)).start()
+        return 0
+
+    lax.fori_loop(1, 8, send_v, 0)
+    taken[g] = given[g]
+
     pick = lax.broadcasted_iota(jnp.int32, (8, 64), 1)
     scale = jnp.exp(decay_ref[...])
 
@@ -201,8 +240,9 @@
             for i in range(4):
                 value = jnp.sum(jnp.where(here, dv_ref[i, h].astype(F32), 0.0), axis=1, keepdims=True)
                 state = factor[2 * i + h : 2 * i + h + 1] * state + value * k[i, h : h + 1, :]
-                y = jnp.sum(state * q[i, h : h + 1, :], axis=1, keepdims=True)
-                ys[2 * i + h] = jnp.where(here, y, ys[2 * i + h])
+                if ys:
+                    y = jnp.sum(state * q[i, h : h + 1, :], axis=1, keepdims=True)
+                    ys[2 * i + h] = jnp.where(here, y, ys[2 * i + h])
             cache[at, h] = state
         return tuple(ys)
 
@@ -210,6 +250,43 @@
     ys = lax.fori_loop(
         0, 64, lambda s, ys: decode_row(s, s, ys), tuple(jnp.zeros((16, 64), F32) for _ in range(8)), unroll=2
     )
+    fresh = lane < 64
+    for p in range(8):
+        fresh = jnp.logical_and(fresh, lane != slot_ref[p])
+    for i in range(4):
+        squares = jnp.zeros((1, 64), F32)
+        parts = []
+        for h in range(2):
+            y = jnp.where(fresh, ys[2 * i + h], 0.0)
+            squares = squares + jnp.sum(y * y, axis=0, keepdims=True)
+            parts.append(y * gated[i, h])
+        parts.append(jnp.broadcast_to(squares, (8, 64)))
+        parts.append(jnp.zeros((HS - 40, 64), F32))
+        zrow[pl.ds(i, 64, stride=4), :] = jnp.concatenate(parts, axis=0).T
+    zmine[...] = zrow[...].T[:40]
+
+    def copy_z(to):
+        return remote(zmine, zbuf.at[g], sz.at[to], rz.at[g], (c, to))
+
+    def arrival_z(frm):
+        return remote(zmine, zbuf.at[frm], sz.at[frm], rz.at[frm], (c, frm))
+
+    def send_z(d, _):
+        copy_z(lax.rem(g + d, 8)).start()
+        return 0
+
+    lax.fori_loop(1, 8, send_z, 0)
+    zbuf[g] = zmine[...]
+
+    to_row = lax.broadcasted_iota(jnp.int32, (256, HS), 0)
+    from_row = lax.broadcasted_iota(jnp.int32, (256, HS), 1)
+    target = jnp.zeros((256, HS), jnp.int32)
+    for p in range(8):
+        target = jnp.where(lax.div(from_row, 16) == p, 4 * slot_ref[p], target)
+    hit = to_row == target + lax.rem(from_row, 4)
+    for n in range(3):
+        kind = lax.rem(lax.div(from_row, 4), 4) == n
+        place[n] = jnp.where(jnp.logical_and(hit, kind), 1.0, 0.0).astype(BF16)
 
     causal = lax.broadcasted_iota(jnp.int32, (HS, HS), 0) >= lax.broadcasted_iota(jnp.int32, (HS, HS), 1)
 
@@ -261,7 +338,6 @@
 
         @pl.when(j != chip)
         def _():
-            copy_2(j).start()
             arrival_1(j).wait_recv()
 
         for r in range(2):
@@ -271,8 +347,47 @@
     lax.fori_loop(0, 8, scan, 0)
     qbuf[chip] = pbuf[chip]
 
-    for r in range(2):
-        fbuf[:, r] = pcur[r].T.reshape(8, 16, HS)
+    def wait_v(d, _):
+        arrival_v(lax.rem(g + d, 8)).wait_recv()
+        return 0
+
+    lax.fori_loop(1, 8, wait_v, 0)
+    columns = jnp.concatenate([taken[n] for n in range(8)], axis=0)
+    mine = slot_ref[g]
+    q, k = dq_ref[mine].astype(F32), dk_ref[mine].astype(F32)
+    step_scale = jnp.sum(jnp.where(pick == mine, scale, 0.0), axis=1, keepdims=True)
+    tall_lane = lax.broadcasted_iota(jnp.int32, (HS, HS), 1)
+    tall = jnp.zeros((HS, HS), F32)
+    for h in range(2):
+        state = pcur[h].T
+        fbuf[:, h] = state.reshape(8, 16, HS)
+        for i in range(4):
+            n = 4 * h + i
+            state = step_scale[2 * i + h : 2 * i + h + 1] * state + columns[:, n : n + 1] * k[i, h : h + 1, :]
+            y = jnp.sum(state * q[i, h : h + 1, :], axis=1, keepdims=True)
+            tall = jnp.where(tall_lane == n, y * columns[:, 8 + n : 9 + n], tall)
+            squares = jnp.sum(y * y, axis=0, keepdims=True)
+            tall = jnp.where(tall_lane == 8 + i, tall + squares, tall)
+    ymine[...] = tall.T[:16]
+
+    def copy_y(to):
+        return remote(ymine, ybuf.at[g], sy.at[to], ry.at[g], (c, to))
+
+    def arrival_y(frm):
+        return remote(ymine, ybuf.at[frm], sy.at[frm], ry.at[frm], (c, frm))
+
+    def send_y(d, _):
+        copy_y(lax.rem(g + d, 8)).start()
+        return 0
+
+    lax.fori_loop(1, 8, send_y, 0)
+
+    def send_2(d, _):
+        copy_2(lax.rem(chip + d, 8)).start()
+        return 0
+
+    lax.fori_loop(1, 8, send_2, 0)
+    ybuf[g] = ymine[...]
 
     def copy_h(to):
         return remote(fbuf.at[to], hbuf.at[g], sh.at[to], rh.at[g], (c, to))
@@ -287,52 +402,18 @@
     lax.fori_loop(1, 8, send_h, 0)
     hbuf[g] = fbuf[g]
 
-    lax.fori_loop(HEADS_AT_SCAN // UNROLL, HEADS_AT_HAND // UNROLL, some, 0)
-
-    def take_h(d, _):
+    def wait_z(d, _):
         frm = lax.rem(g + d, 8)
-        arrival_h(frm).wait_recv()
+        arrival_z(frm).wait_recv()
         arrival_w(frm).wait_recv()
         return 0
 
-    lax.fori_loop(1, 8, take_h, 0)
-    cache[64:72] = hbuf[...]
-    ys = lax.fori_loop(0, 8, lambda p, ys: decode_row(64 + p, slot_ref[p], ys), ys, unroll=2)
-    for i in range(4):
-        squares = jnp.zeros((1, 64), F32)
-        parts = []
-        for h in range(2):
-            y = ys[2 * i + h]
-            squares = squares + jnp.sum(y * y, axis=0, keepdims=True)
-            parts.append(y * gain_ref[h] * jax.nn.sigmoid(gate_ref[i, h].astype(F32)))
-        parts.append(jnp.broadcast_to(squares, (8, 64)))
-        parts.append(jnp.zeros((HS - 40, 64), F32))
-        zrow[pl.ds(i, 64, stride=4), :] = jnp.concatenate(parts, axis=0).T
-    zmine[...] = zrow[...].T[:40]
-
-    def copy_z(to):
-        return remote(zmine, zbuf.at[g], sz.at[to], rz.at[g], (c, to))
-
-    def arrival_z(frm):
-        return remote(zmine, zbuf.at[frm], sz.at[frm], rz.at[frm], (c, frm))
-
-    def send_z(d, _):
-        copy_z(lax.rem(g + d, 8)).start()
-        return 0
-
-    lax.fori_loop(1, 8, send_z, 0)
-    zbuf[g] = zmine[...]
-
-    for frm in range(8):
-        wt[frm * 32 : (frm + 1) * 32, :] = wr[frm].astype(BF16)
-    lax.fori_loop(HEADS_AT_HAND // UNROLL, H // UNROLL, some, 0)
-
-    def wait_z(d, _):
-        arrival_z(lax.rem(g + d, 8)).wait_recv()
-        return 0
-
     lax.fori_loop(1, 8, wait_z, 0)
-    z = jnp.concatenate([zbuf[n, 0:32, :] for n in range(8)], axis=0).T
+    for h in range(2):
+        for frm in range(8):
+            at = h * HS + frm * 16
+            wt[at : at + 16, :] = wr[frm, h * 16 : (h + 1) * 16, :].astype(BF16)
+    z = jnp.concatenate([zbuf[n, 16 * h : 16 * h + 16, :] for h in range(2) for n in range(8)], axis=0).T
     squares = zbuf[0, 32:40, :]
     for n in range(1, 8):
         squares = squares + zbuf[n, 32:40, :]
@@ -347,8 +428,29 @@
     both = squares.reshape(8, 2, 16, HS)
     for k in range(2):
         part[k, :, :, 768:896] = both[:, k]
+    lax.fori_loop(HEADS_AT_SCAN // UNROLL, HEADS_AT_GATHER // UNROLL, some, 0)
+
+    def wait_y(d, _):
+        arrival_y(lax.rem(g + d, 8)).wait_recv()
+        return 0
+
+    lax.fori_loop(1, 8, wait_y, 0)
+    hi, lo = split(ybuf[...].reshape(HS, HS))
+    squares = (dot(place[2], hi) + dot(place[2], lo)).reshape(8, 2, 16, HS)
+    hi = [dot(place[h], hi).astype(BF16) for h in range(2)]
+    lo = [dot(place[h], lo).astype(BF16) for h in range(2)]
+    z = jnp.concatenate([jnp.concatenate(hi, axis=1), jnp.concatenate(lo, axis=1)], axis=0)
+    for n in range(3):
+        span = slice(n * 256, (n + 1) * 256)
+        both = dot(z, wt[:, span])
+        both = (both[:256] + both[256:]).reshape(8, 2, 16, 256)
+        for k in range(2):
+            part[k, :, :, span] = part[k, :, :, span] + both[:, k]
+    for k in range(2):
+        part[k, :, :, 768:896] = part[k, :, :, 768:896] + squares[:, k]
     copy_c = remote(part.at[other], half, sc, rc, partner)
     copy_c.start()
+    lax.fori_loop(HEADS_AT_GATHER // UNROLL, HEADS_AT_SUM // UNROLL, some, 0)
 
     def copy_b(m):
         return remote(obuf.at[pl.ds(4 * m, 4)], states.at[core, pl.ds(4 * m, 4)], sb.at[m], rb.at[m], partner)
@@ -374,8 +476,6 @@
         copy_b(m).start()
         return 0
 
-    lax.fori_loop(0, 4, spread, 0)
-
     copy_c.wait_recv()
     half[...] = half[...] + part[core]
 
@@ -391,6 +491,10 @@
 
     lax.fori_loop(1, 8, send_p, 0)
     take[chip] = half[chip]
+    lax.fori_loop(0, 4, spread, 0)
+
+
+    lax.fori_loop(HEADS_AT_SUM // UNROLL, H // UNROLL, some, 0)
 
     def take_b(m, _):
         arrival_b(m).wait_recv()
@@ -445,6 +549,14 @@
     lax.fori_loop(1, 8, send_d, 0)
     last[g] = done[g]
 
+    def take_h(d, _):
+        arrival_h(lax.rem(g + d, 8)).wait_recv()
+        return 0
+
+    lax.fori_loop(1, 8, take_h, 0)
+    cache[64:72] = hbuf[...]
+    lax.fori_loop(0, 8, lambda p, ys: decode_row(64 + p, slot_ref[p], ys), ())
+
     def merge(s, _):
         at = s
         for p in range(8):
@@ -487,6 +599,8 @@
         copy_h(to).wait_send()
         copy_z(to).wait_send()
         copy_d(to).wait_send()
+        copy_v(to).wait_send()
+        copy_y(to).wait_send()
         return 0
 
     lax.fori_loop(1, 8, finish, 0)
@@ -543,10 +657,17 @@
             pltpu.VMEM((8, 16, 896), F32),
             pltpu.VMEM((8, 2, 768), F32),
             pltpu.VMEM((8, 2, 768), F32),
+            pltpu.VMEM((4, 2, 16, 64), F32),
+            pltpu.VMEM((8, 16, HS), F32),
+            pltpu.VMEM((8, 16, HS), F32),
+            pltpu.VMEM((16, HS), F32),
+            pltpu.VMEM((8, 16, HS), F32),
+            pltpu.VMEM((3, 256, HS), BF16),
             dma((3, 2)), dma, dma, dma((2,)),
             dma((2,)), dma((2,)), dma((8,)), dma((8,)), dma((8,)), dma((8,)),
             dma((4,)), dma((4,)), dma((8,)), dma((8,)), dma((8,)), dma((8,)),
             dma((8,)), dma((8,)), dma, dma, dma((8,)), dma((8,)), dma((8,)), dma((8,)),
+            dma((8,)), dma((8,)), dma((8,)), dma((8,)),
         ],
         compiler_params=pltpu.CompilerParams(
             collective_id=0, has_side_effects=True, vmem_limit_bytes=VMEM_LIMIT
@@ -565,7 +686,7 @@
         jnp.transpose(decode_values, (1, 2, 3, 0)),
         jnp.transpose(decode_gate, (1, 2, 3, 0)),
         jnp.transpose(decode_decay, (1, 2, 0)).reshape(8, 64),
-        norm_gain[:, :, None],
+        norm_gain,
     )
     return prefill_out[None], jnp.swapaxes(cache, 2, 3), decoded
 

time: 82.3 us -> 74.6 us (0.906)
  Pallas kernels: 73 us -> 67.2 us
  local copies, waits for them, and re-layouts: 7.97 us -> 6.6 us
    pallas_call x1, Pallas kernels: 73 us -> 67.2 us  [per_device(): pl.pallas_call(kernel, name='lightning', out_shape=(jax.ShapeDtypeStruct(...]
    broadcast_in_dim x1 -> x0, local copies, waits for them, and re-layouts: 1.37 us -> none  [per_device(): norm_gain[:, :, None]]
where the time goes in v4:
time: 74.6 us; the launch traced here: 74.5 us
  Pallas kernels  67.2 us (90%)
  local copies, waits for them, and re-layouts  6.6 us (9%)
    pallas_call x1, Pallas kernels, per_device(): pl.pallas_call(kernel, name='lightning', out_shape=(jax.ShapeDtypeStruct(...  67.2 us
    unnamed x7, local copies, waits for them, and re-layouts  6.6 us

profile of v4, /device:TPU:0, one launch (start us, length us, event | category | flops | bytes accessed | tf_op | source)
XLA Modules:
  0.0 74.5 jit_solution(15244171576647558337)
XLA Ops:
  0.6 67.2 %lightning.1 = (bf16[512,32,128]{2,1,0:T(8,128)(2,1)}, f32[64,2,16,128]{3,2,1,0:T(8,128)}, f32[2,6144]{1,0:T(2,128)}) custom-call(s32[8]{0:T(128)} %slot_ref.1, bf16[512,32,128]{2,1,0:T(8,128)(2,1)} %bitcast.16, bf16[512,32,128]{2,1,0:T(8,128)(2,1)} %bitcast.17, bf16[512,32,128]{2,1,0:T(8,128)(2,1)} %bitcast.18, f32[32,512]{1,0:T(8,128)} %bitcast.24, ...), custom_call_target="tpu_custom_call" | custom-call | tf_op jit(solution)/shard_map/lightning/pallas_call | solution.py:615
  67.9 0.0 copy-start
  67.9 0.0 copy-start.1
  67.9 5.0 %copy.20 = bf16[1,512,32,128]{3,2,1,0:T(8,128)(2,1)} copy(bf16[1,512,32,128]{3,2,1,0:T(8,128)(2,1)} %bitcast.19) | data formatting | bytes 8388608
  72.9 0.0 copy-done
  72.9 1.0 %copy.21 = f32[64,2,128,16]{2,3,1,0:T(8,128)} copy(f32[64,2,128,16]{2,3,1,0:T(8,128)S(1)} %bitcast.21) | data formatting | bytes 2097152
  73.8 0.0 copy-done.1
  73.9 0.6 copy.22
Async XLA Ops:
  67.9 5.0 %copy-start = (f32[64,2,16,128]{3,2,1,0:T(8,128)S(1)}, f32[64,2,16,128]{3,2,1,0:T(8,128)}, u32[]{:S(2)}) copy-start(f32[64,2,16,128]{3,2,1,0:T(8,128)} %get-tuple-element.7) | copy-start | bytes 3145732
  67.9 6.0 %copy-start.1 = (f32[2,6144]{1,0:T(2,128)S(1)}, f32[2,6144]{1,0:T(2,128)}, u32[]{:S(2)}) copy-start(f32[2,6144]{1,0:T(2,128)} %get-tuple-element.14) | copy-start | bytes 147460

commit v5 on v4

--- a/solution.py
+++ b/solution.py
@@ -11,7 +11,7 @@
 MESH = pl.DeviceIdType.MESH
 F32 = jnp.float32
 BF16 = jnp.bfloat16
-VMEM_LIMIT = 60 * 1024 * 1024
+VMEM_LIMIT = 54 * 1024 * 1024
 T = 512
 CH = 128
 ROWS = 136
@@ -42,11 +42,11 @@
 
 def kernel(
     slot_ref, q_hbm, k_hbm, v_hbm, dec_ref, start_ref, w_ref, cache_hbm, dq_ref, dk_ref, dv_ref, gate_ref, decay_ref, gain_ref,
-    out_hbm, new_hbm, decoded_ref,
+    out_ref, new_ref, decoded_ref,
     raw, qh, kt, vh, cum2, cum, ec, s_ref, xbuf, tbuf, rbuf, pbuf, qbuf, obuf, states, pcur, fbuf, hbuf, wf, wr, wt, att,
-    wide, outs, cache, merged, zrow, zmine, zbuf, part, half, take, done, last,
+    wide, cache, zrow, zmine, zbuf, part, half, take, done, last,
     gated, given, taken, ymine, ybuf, place,
-    load_sem, cache_sem, new_sem, out_sem, sa, ra, s1, r1, s2, r2, sb, rb, sh, rh, sw, rw, sz, rz, sc, rc, sp, rp, sd, rd, sv, rv, sy, ry,
+    load_sem, cache_sem, sa, ra, s1, r1, s2, r2, sb, rb, sh, rh, sw, rw, sz, rz, sc, rc, sp, rp, sd, rd, sv, rv, sy, ry,
 ):
     c, g = lax.axis_index("ctx"), lax.axis_index("grp")
     core, chip = lax.rem(c, 2), lax.div(c, 2)
@@ -61,13 +61,11 @@
 
     def load(which, hbm, row):
         heads = pl.ds(pl.multiple_of(16 * row, 16), 16)
-        return pltpu.make_async_copy(hbm.at[:, heads], raw.at[which, row], load_sem.at[which, row])
+        return pltpu.make_async_copy(hbm.at[:, heads], raw.at[which % 2, row], load_sem.at[which, row])
 
     for row in rows:
         load(0, k_hbm, row).start()
         load(1, v_hbm, row).start()
-    for row in rows:
-        load(2, q_hbm, row).start()
     cache_load = pltpu.make_async_copy(cache_hbm, cache.at[pl.ds(0, 64)], cache_sem)
     cache_load.start()
 
@@ -92,7 +90,7 @@
     ec[...] = jnp.concatenate([jnp.exp(total), jnp.zeros((HS - H, T), F32)], axis=0).T
 
     def heads_first(which, row, at):
-        return jnp.swapaxes(raw[which, row, pl.ds(at * CH, CH)], 0, 1)
+        return jnp.swapaxes(raw[which % 2, row, pl.ds(at * CH, CH)], 0, 1)
 
     def relay_kv(row):
         load(0, k_hbm, row).wait()
@@ -171,8 +169,10 @@
     wr[g] = wf[g]
 
     relay_kv(rows[0])
+    load(2, q_hbm, rows[0]).start()
     local_states(rows[0])
     relay_kv(rows[1])
+    load(2, q_hbm, rows[1]).start()
     copy_a(rows[0]).wait_recv()
     lax.fori_loop(0, 4, send_total(rows[0]), 0)
     local_states(rows[1])
@@ -383,10 +383,15 @@
     lax.fori_loop(1, 8, send_y, 0)
 
     def send_2(d, _):
-        copy_2(lax.rem(chip + d, 8)).start()
-        return 0
-
-    lax.fori_loop(1, 8, send_2, 0)
+        copy_2(4 * own_row + lax.rem(x + d, 4)).start()
+        return 0
+
+    def send_2_across(d, _):
+        copy_2(4 * rows[0] + lax.rem(x + d, 4)).start()
+        return 0
+
+    lax.fori_loop(0, 4, send_2_across, 0)
+    lax.fori_loop(1, 4, send_2, 0)
     ybuf[g] = ymine[...]
 
     def copy_h(to):
@@ -506,10 +511,7 @@
         wide[h, :, 0:HS] = hi
         wide[h, :, HS:] = lo
 
-    def out_copy(at, slot):
-        return pltpu.make_async_copy(outs.at[slot], out_hbm.at[pl.ds(at * CH, CH)], out_sem.at[slot])
-
-    for at in range(T // CH):
+    def finish_chunk(at):
         span = slice(at * CH, (at + 1) * CH)
         squares = jnp.zeros((CH, HS), F32)
         for h in range(H):
@@ -519,10 +521,10 @@
             squares = squares + field * field
         mean = jnp.sum(squares, axis=1, keepdims=True) / (H * HS)
         factor = jnp.broadcast_to(lax.rsqrt(mean + 1e-06), (CH, HS))
-        if at >= 2:
-            out_copy(at - 2, at % 2).wait()
-        outs[at % 2] = jnp.swapaxes((att[:, span, :] * factor[None]).astype(BF16), 0, 1)
-        out_copy(at, at % 2).start()
+        out_ref[span] = jnp.swapaxes((att[:, span, :] * factor[None]).astype(BF16), 0, 1)
+
+    for at in range(2):
+        finish_chunk(at)
 
     def wait_p(d, _):
         arrival_p(lax.rem(chip + d, 8)).wait_recv()
@@ -549,6 +551,9 @@
     lax.fori_loop(1, 8, send_d, 0)
     last[g] = done[g]
 
+    for at in range(2, T // CH):
+        finish_chunk(at)
+
     def take_h(d, _):
         arrival_h(lax.rem(g + d, 8)).wait_recv()
         return 0
@@ -561,12 +566,10 @@
         at = s
         for p in range(8):
             at = jnp.where(slot_ref[p] == s, 64 + p, at)
-        merged[s] = cache[at]
+        new_ref[s] = cache[at]
         return 0
 
     lax.fori_loop(0, 64, merge, 0)
-    new_copy = pltpu.make_async_copy(merged, new_hbm, new_sem)
-    new_copy.start()
 
     def wait_d(d, _):
         arrival_d(lax.rem(g + d, 8)).wait_recv()
@@ -576,9 +579,6 @@
     for n in range(8):
         decoded_ref[:, n * 768 : (n + 1) * 768] = last[n]
 
-    out_copy(2, 0).wait()
-    out_copy(3, 1).wait()
-    new_copy.wait()
     for row in rows:
         copy_a(row).wait_send()
     copy_c.wait_send()
@@ -612,18 +612,19 @@
 ):
     dma = pltpu.SemaphoreType.DMA
     hbm, vmem = pl.BlockSpec(memory_space=pl.ANY), pl.BlockSpec(memory_space=pltpu.VMEM)
+    results = (
+        jax.ShapeDtypeStruct((T, H, HS), BF16),
+        jax.ShapeDtypeStruct((64, 2, 16, HS), F32),
+        jax.ShapeDtypeStruct((2, 6144), F32),
+    )
     prefill_out, cache, decoded = pl.pallas_call(
         kernel,
         name="lightning",
-        out_shape=(
-            jax.ShapeDtypeStruct((T, H, HS), BF16),
-            jax.ShapeDtypeStruct((64, 2, 16, HS), F32),
-            jax.ShapeDtypeStruct((2, 6144), F32),
-        ),
+        out_shape=tuple(pltpu.VMEM(x.shape, x.dtype) for x in results),
         in_specs=[pl.BlockSpec(memory_space=pltpu.SMEM), hbm, hbm, hbm, vmem, vmem, vmem, hbm] + [vmem] * 6,
-        out_specs=(hbm, hbm, vmem),
+        out_specs=(vmem, vmem, vmem),
         scratch_shapes=[
-            pltpu.VMEM((3, 2, T, 16, HS), BF16),
+            pltpu.VMEM((2, 2, T, 16, HS), BF16),
             pltpu.VMEM((H, T, HS), BF16),
             pltpu.VMEM((H, HS, T), BF16),
             pltpu.VMEM((H, T, HS), BF16),
@@ -646,9 +647,7 @@
             pltpu.VMEM((256, 768), BF16),
             pltpu.VMEM((H, T, HS), F32),
             pltpu.VMEM((H, HS, 2 * HS), BF16),
-            pltpu.VMEM((2, CH, H, HS), BF16),
             pltpu.VMEM((72, 2, 16, HS), F32),
-            pltpu.VMEM((64, 2, 16, HS), F32),
             pltpu.VMEM((256, HS), F32),
             pltpu.VMEM((40, 256), F32),
             pltpu.VMEM((8, 40, 256), F32),
@@ -663,7 +662,7 @@
             pltpu.VMEM((16, HS), F32),
             pltpu.VMEM((8, 16, HS), F32),
             pltpu.VMEM((3, 256, HS), BF16),
-            dma((3, 2)), dma, dma, dma((2,)),
+            dma((3, 2)), dma,
             dma((2,)), dma((2,)), dma((8,)), dma((8,)), dma((8,)), dma((8,)),
             dma((4,)), dma((4,)), dma((8,)), dma((8,)), dma((8,)), dma((8,)),
             dma((8,)), dma((8,)), dma, dma, dma((8,)), dma((8,)), dma((8,)), dma((8,)),

time: 74.6 us -> 68.5 us (0.918)
  Pallas kernels: 67.2 us -> 64.1 us
  local copies, waits for them, and re-layouts: 6.6 us -> 3.6 us
    pallas_call x1, Pallas kernels: 67.2 us -> 64.1 us  [per_device(): pl.pallas_call(kernel, name='lightning', out_shape=tuple((pltpu.VMEM(x.sh...]
    unnamed x7 -> x3, local copies, waits for them, and re-layouts: 6.6 us -> 3.6 us
where the time goes in v5:
time: 68.5 us; the launch traced here: 68.3 us
  Pallas kernels  64.1 us (94%)
  local copies, waits for them, and re-layouts  3.6 us (5%)
    pallas_call x1, Pallas kernels, per_device(): pl.pallas_call(kernel, name='lightning', out_shape=tuple((pltpu.VMEM(x.sh...  64.1 us
    unnamed x3, local copies, waits for them, and re-layouts  3.6 us

profile of v5, /device:TPU:0, one launch (start us, length us, event | category | flops | bytes accessed | tf_op | source)
XLA Modules:
  0.0 68.3 jit_solution(18269979617287527534)
XLA Ops:
  0.6 64.1 %lightning.1 = (bf16[512,32,128]{2,1,0:T(8,128)(2,1)S(1)}, f32[64,2,16,128]{3,2,1,0:T(8,128)S(1)}, f32[2,6144]{1,0:T(2,128)S(1)}) custom-call(s32[8]{0:T(128)} %slot_ref.1, bf16[512,32,128]{2,1,0:T(8,128)(2,1)} %bitcast.18, bf16[512,32,128]{2,1,0:T(8,128)(2,1)} %bitcast.19, bf16[512,32,128]{2,1,0:T(8,128)(2,1)} %bitcast.20, f32[32,512]{1,0:T(8,128)} %bitcast.24, ...), custom_call_target="tpu_custom_call" | custom-call | tf_op jit(solution)/shard_map/lightning/pallas_call | solution.py:620
  64.7 2.0 %copy.20 = bf16[1,512,32,128]{3,2,1,0:T(8,128)(2,1)} copy(bf16[1,512,32,128]{3,2,1,0:T(8,128)(2,1)S(1)} %bitcast.16) | data formatting | bytes 8388608
  66.7 1.0 %copy.21 = f32[64,2,128,16]{2,3,1,0:T(8,128)} copy(f32[64,2,128,16]{2,3,1,0:T(8,128)S(1)} %bitcast.17) | data formatting | bytes 2097152
  67.7 0.6 copy.22

commit v6 on v5

--- a/solution.py
+++ b/solution.py
@@ -45,8 +45,8 @@
     out_ref, new_ref, decoded_ref,
     raw, qh, kt, vh, cum2, cum, ec, s_ref, xbuf, tbuf, rbuf, pbuf, qbuf, obuf, states, pcur, fbuf, hbuf, wf, wr, wt, att,
     wide, cache, zrow, zmine, zbuf, part, half, take, done, last,
-    gated, given, taken, ymine, ybuf, place,
-    load_sem, cache_sem, sa, ra, s1, r1, s2, r2, sb, rb, sh, rh, sw, rw, sz, rz, sc, rc, sp, rp, sd, rd, sv, rv, sy, ry,
+    gated, given, taken, ymine, ybuf, place, row_total, twin_total, start_all, row_start,
+    load_sem, cache_sem, sa, ra, s1, r1, s2, r2, sb, rb, sh, rh, sw, rw, sz, rz, sc, rc, sp, rp, sd, rd, sv, rv, sy, ry, st, rt, ss, rs,
 ):
     c, g = lax.axis_index("ctx"), lax.axis_index("grp")
     core, chip = lax.rem(c, 2), lax.div(c, 2)
@@ -58,6 +58,13 @@
 
     x, own_row = lax.rem(chip, 4), lax.div(chip, 4)
     rows = (1 - own_row, own_row)
+    twin = peer(4 * rows[0] + x)
+
+    def in_row(j):
+        return peer(4 * own_row + lax.rem(j, 4))
+
+    def mine_of(j):
+        return 4 * lax.div(j, 4) + x
 
     def load(which, hbm, row):
         heads = pl.ds(pl.multiple_of(16 * row, 16), 16)
@@ -120,10 +127,10 @@
         return remote(s_ref.at[other, part], xbuf.at[part], sa.at[row], ra.at[row], partner)
 
     def copy_1(j):
-        return remote(tbuf.at[j], rbuf.at[chip], s1.at[j], r1.at[chip], peer(j))
+        return remote(tbuf.at[j], rbuf.at[mine_of(j)], s1.at[j], r1.at[mine_of(j)], in_row(j))
 
     def arrival_1(j):
-        return remote(tbuf.at[j], rbuf.at[j], s1.at[j], r1.at[j], peer(j))
+        return remote(tbuf.at[j], rbuf.at[j], s1.at[j], r1.at[j], in_row(j))
 
     def chip_total(j):
         for r in range(2):
@@ -165,7 +172,17 @@
         copy_w(lax.rem(g + d, 8)).start()
         return 0
 
-    lax.fori_loop(1, 8, send_w, 0)
+    def send_w_odd(n, _):
+        return send_w(2 * n + 1, 0)
+
+    def send_w_even(n, _):
+        return send_w(2 * n, 0)
+
+    lax.fori_loop(0, 4, send_w_odd, 0)
+    lax.fori_loop(1, 4, send_w_even, 0)
+    copy_s = remote(start_ref, start_all.at[own_row], ss, rs, twin)
+    copy_s.start()
+    start_all[own_row] = start_ref[...]
     wr[g] = wf[g]
 
     relay_kv(rows[0])
@@ -174,12 +191,28 @@
     relay_kv(rows[1])
     load(2, q_hbm, rows[1]).start()
     copy_a(rows[0]).wait_recv()
-    lax.fori_loop(0, 4, send_total(rows[0]), 0)
+    lax.fori_loop(1, 4, send_total(rows[0]), 0)
     local_states(rows[1])
     copy_a(rows[1]).wait_recv()
     lax.fori_loop(1, 4, send_total(rows[1]), 0)
-    chip_total(chip)
-    rbuf[chip] = tbuf[chip]
+    for row in rows:
+        chip_total(4 * row + x)
+        rbuf[4 * row + x] = tbuf[4 * row + x]
+
+    def fold(row):
+        for d in range(1, 4):
+            arrival_1(4 * row + lax.rem(x + d, 4)).wait_recv()
+        for r in range(2):
+            total = rbuf[4 * row, r]
+            for n in range(1, 4):
+                term = rbuf[4 * row + n, r]
+                total = jnp.concatenate(
+                    [jnp.exp(term[HS : HS + 1]) * total[:HS] + term[:HS], total[HS:] + term[HS:]], axis=0
+                )
+            row_total[row, r] = total
+
+    def copy_t(row):
+        return remote(row_total.at[row], twin_total.at[row], st.at[row], rt.at[row], twin)
 
     for row in rows:
         load(2, q_hbm, row).wait()
@@ -248,8 +281,11 @@
 
     cache_load.wait()
     ys = lax.fori_loop(
-        0, 64, lambda s, ys: decode_row(s, s, ys), tuple(jnp.zeros((16, 64), F32) for _ in range(8)), unroll=2
+        0, 32, lambda s, ys: decode_row(s, s, ys), tuple(jnp.zeros((16, 64), F32) for _ in range(8)), unroll=2
     )
+    fold(rows[0])
+    copy_t(rows[0]).start()
+    ys = lax.fori_loop(32, 64, lambda s, ys: decode_row(s, s, ys), ys, unroll=2)
     fresh = lane < 64
     for p in range(8):
         fresh = jnp.logical_and(fresh, lane != slot_ref[p])
@@ -326,26 +362,31 @@
     lax.fori_loop(0, HEADS_AT_SCAN // UNROLL, some, 0)
 
     def copy_2(j):
-        return remote(pbuf.at[j], qbuf.at[chip], s2.at[j], r2.at[chip], peer(j))
+        return remote(pbuf.at[j], qbuf.at[mine_of(j)], s2.at[j], r2.at[mine_of(j)], in_row(j))
 
     def arrival_2(j):
-        return remote(pbuf.at[j], qbuf.at[j], s2.at[j], r2.at[j], peer(j))
-
-    pcur[...] = start_ref[...]
-
-    def scan(j, _):
-        pbuf[j] = pcur[...]
-
-        @pl.when(j != chip)
+        return remote(pbuf.at[j], qbuf.at[j], s2.at[j], r2.at[j], in_row(j))
+
+    fold(rows[1])
+
+    @pl.when(own_row == 0)
+    def _():
+        copy_t(0).start()
+
+    copy_t(own_row).wait_recv()
+
+    def through(total, state):
+        return jnp.exp(total[HS : HS + 1]) * state + total[:HS]
+
+    for r in range(2):
+
+        @pl.when(own_row == 0)
         def _():
-            arrival_1(j).wait_recv()
-
-        for r in range(2):
-            pcur[r] = jnp.exp(rbuf[j, r, HS : HS + 1, :]) * pcur[r] + rbuf[j, r, 0:HS, :]
-        return 0
-
-    lax.fori_loop(0, 8, scan, 0)
-    qbuf[chip] = pbuf[chip]
+            pcur[r] = through(twin_total[own_row, r], through(row_total[own_row, r], start_ref[r]))
+
+        @pl.when(own_row == 1)
+        def _():
+            pcur[r] = through(row_total[own_row, r], through(twin_total[own_row, r], start_ref[r]))
 
     def wait_v(d, _):
         arrival_v(lax.rem(g + d, 8)).wait_recv()
@@ -382,16 +423,34 @@
 
     lax.fori_loop(1, 8, send_y, 0)
 
-    def send_2(d, _):
-        copy_2(4 * own_row + lax.rem(x + d, 4)).start()
-        return 0
-
-    def send_2_across(d, _):
-        copy_2(4 * rows[0] + lax.rem(x + d, 4)).start()
-        return 0
-
-    lax.fori_loop(0, 4, send_2_across, 0)
-    lax.fori_loop(1, 4, send_2, 0)
+    remote(start_ref, start_all.at[rows[0]], ss, rs, twin).wait_recv()
+
+    @pl.when(own_row == 0)
+    def _():
+        row_start[...] = start_all[...]
+
+    @pl.when(own_row == 1)
+    def _():
+        copy_t(0).wait_recv()
+        for row in range(2):
+            for r in range(2):
+                row_start[row, r] = through(twin_total[row, r], start_all[row, r])
+
+    def before_chip(j, _):
+        row = lax.div(j, 4)
+        pbuf[j] = row_start[row]
+
+        @pl.when(lax.rem(j, 4) != x)
+        def _():
+            copy_2(j).start()
+
+        for r in range(2):
+            row_start[row, r] = through(rbuf[j, r], row_start[row, r])
+        return 0
+
+    lax.fori_loop(0, 8, before_chip, 0)
+    for row in range(2):
+        qbuf[4 * row + x] = pbuf[4 * row + x]
     ybuf[g] = ymine[...]
 
     def copy_h(to):
@@ -467,7 +526,7 @@
         for n in range(2):
             j = 2 * m + n
 
-            @pl.when(j != chip)
+            @pl.when(lax.rem(j, 4) != x)
             def _():
                 arrival_2(j).wait_recv()
 
@@ -591,8 +650,6 @@
 
     def finish(d, _):
         j = lax.rem(chip + d, 8)
-        copy_1(j).wait_send()
-        copy_2(j).wait_send()
         copy_p(j).wait_send()
         to = lax.rem(g + d, 8)
         copy_w(to).wait_send()
@@ -604,6 +661,21 @@
         return 0
 
     lax.fori_loop(1, 8, finish, 0)
+
+    def finish_rows(d, _):
+        for row in range(2):
+            j = 4 * row + lax.rem(x + d, 4)
+            copy_1(j).wait_send()
+            copy_2(j).wait_send()
+        return 0
+
+    lax.fori_loop(1, 4, finish_rows, 0)
+    copy_s.wait_send()
+    copy_t(rows[0]).wait_send()
+
+    @pl.when(own_row == 0)
+    def _():
+        copy_t(0).wait_send()
 
 
 def per_device(
@@ -662,11 +734,15 @@
             pltpu.VMEM((16, HS), F32),
             pltpu.VMEM((8, 16, HS), F32),
             pltpu.VMEM((3, 256, HS), BF16),
+            pltpu.VMEM((2, 2, ROWS, HS), F32),
+            pltpu.VMEM((2, 2, ROWS, HS), F32),
+            pltpu.VMEM((2, 2, HS, HS), F32),
+            pltpu.VMEM((2, 2, HS, HS), F32),
             dma((3, 2)), dma,
             dma((2,)), dma((2,)), dma((8,)), dma((8,)), dma((8,)), dma((8,)),
             dma((4,)), dma((4,)), dma((8,)), dma((8,)), dma((8,)), dma((8,)),
             dma((8,)), dma((8,)), dma, dma, dma((8,)), dma((8,)), dma((8,)), dma((8,)),
-            dma((8,)), dma((8,)), dma((8,)), dma((8,)),
+            dma((8,)), dma((8,)), dma((8,)), dma((8,)), dma((2,)), dma((2,)), dma, dma,
         ],
         compiler_params=pltpu.CompilerParams(
             collective_id=0, has_side_effects=True, vmem_limit_bytes=VMEM_LIMIT

time: 68.5 us -> 65.7 us (0.959)
  the two profiles are of different devices: /device:TPU:0 before, /device:TPU:22 now
where the time goes in v6:
time: 65.7 us; the launch traced here: 65.6 us
  Pallas kernels  61.3 us (93%)
  local copies, waits for them, and re-layouts  3.6 us (5%)
    pallas_call x1, Pallas kernels, per_device(): pl.pallas_call(kernel, name='lightning', out_shape=tuple((pltpu.VMEM(x.sh...  61.3 us
    unnamed x3, local copies, waits for them, and re-layouts  3.6 us

profile of v6, /device:TPU:22, one launch (start us, length us, event | category | flops | bytes accessed | tf_op | source)
XLA Modules:
  0.0 65.6 jit_solution(2839418168219599187)
XLA Ops:
  0.6 61.3 %lightning.1 = (bf16[512,32,128]{2,1,0:T(8,128)(2,1)S(1)}, f32[64,2,16,128]{3,2,1,0:T(8,128)S(1)}, f32[2,6144]{1,0:T(2,128)S(1)}) custom-call(s32[8]{0:T(128)} %slot_ref.1, bf16[512,32,128]{2,1,0:T(8,128)(2,1)} %bitcast.18, bf16[512,32,128]{2,1,0:T(8,128)(2,1)} %bitcast.19, bf16[512,32,128]{2,1,0:T(8,128)(2,1)} %bitcast.20, f32[32,512]{1,0:T(8,128)} %bitcast.24, ...), custom_call_target="tpu_custom_call" | custom-call | tf_op jit(solution)/shard_map/lightning/pallas_call | solution.py:692
  62.0 2.0 %copy.20 = bf16[1,512,32,128]{3,2,1,0:T(8,128)(2,1)} copy(bf16[1,512,32,128]{3,2,1,0:T(8,128)(2,1)S(1)} %bitcast.16) | data formatting | bytes 8388608
  64.0 1.0 %copy.21 = f32[64,2,128,16]{2,3,1,0:T(8,128)} copy(f32[64,2,128,16]{2,3,1,0:T(8,128)S(1)} %bitcast.17) | data formatting | bytes 2097152
  65.0 0.6 copy.22

commit v7 on v6

--- a/solution.py
+++ b/solution.py
@@ -66,13 +66,17 @@
     def mine_of(j):
         return 4 * lax.div(j, 4) + x
 
-    def load(which, hbm, row):
+    def load(which, hbm, row, at):
         heads = pl.ds(pl.multiple_of(16 * row, 16), 16)
-        return pltpu.make_async_copy(hbm.at[:, heads], raw.at[which % 2, row], load_sem.at[which, row])
+        span = pl.ds(at * CH, CH)
+        return pltpu.make_async_copy(
+            hbm.at[span, heads], raw.at[which % 2, row, span], load_sem.at[which, row, at]
+        )
 
     for row in rows:
-        load(0, k_hbm, row).start()
-        load(1, v_hbm, row).start()
+        for at in range(T // CH):
+            load(1, v_hbm, row, at).start()
+            load(0, k_hbm, row, at).start()
     cache_load = pltpu.make_async_copy(cache_hbm, cache.at[pl.ds(0, 64)], cache_sem)
     cache_load.start()
 
@@ -100,10 +104,9 @@
         return jnp.swapaxes(raw[which % 2, row, pl.ds(at * CH, CH)], 0, 1)
 
     def relay_kv(row):
-        load(0, k_hbm, row).wait()
-        load(1, v_hbm, row).wait()
-
         def chunk(at, _):
+            load(1, v_hbm, row, at).wait()
+            load(0, k_hbm, row, at).wait()
             span = pl.ds(pl.multiple_of(at * CH, CH), CH)
             vh[pl.ds(16 * row, 16), span, :] = heads_first(1, row, at)
             block = heads_first(0, row, at)
@@ -186,10 +189,12 @@
     wr[g] = wf[g]
 
     relay_kv(rows[0])
-    load(2, q_hbm, rows[0]).start()
+    for at in range(T // CH):
+        load(2, q_hbm, rows[0], at).start()
     local_states(rows[0])
     relay_kv(rows[1])
-    load(2, q_hbm, rows[1]).start()
+    for at in range(T // CH):
+        load(2, q_hbm, rows[1], at).start()
     copy_a(rows[0]).wait_recv()
     lax.fori_loop(1, 4, send_total(rows[0]), 0)
     local_states(rows[1])
@@ -215,9 +220,9 @@
         return remote(row_total.at[row], twin_total.at[row], st.at[row], rt.at[row], twin)
 
     for row in rows:
-        load(2, q_hbm, row).wait()
 
         def relay_q(at, _):
+            load(2, q_hbm, row, at).wait()
             span = pl.ds(pl.multiple_of(at * CH, CH), CH)
             qh[pl.ds(16 * row, 16), span, :] = heads_first(2, row, at)
             return 0
@@ -555,10 +560,8 @@
 
     lax.fori_loop(1, 8, send_p, 0)
     take[chip] = half[chip]
+    lax.fori_loop(HEADS_AT_SUM // UNROLL, H // UNROLL, some, 0)
     lax.fori_loop(0, 4, spread, 0)
-
-
-    lax.fori_loop(HEADS_AT_SUM // UNROLL, H // UNROLL, some, 0)
 
     def take_b(m, _):
         arrival_b(m).wait_recv()
@@ -738,7 +741,7 @@
             pltpu.VMEM((2, 2, ROWS, HS), F32),
             pltpu.VMEM((2, 2, HS, HS), F32),
             pltpu.VMEM((2, 2, HS, HS), F32),
-            dma((3, 2)), dma,
+            dma((3, 2, T // CH)), dma,
             dma((2,)), dma((2,)), dma((8,)), dma((8,)), dma((8,)), dma((8,)),
             dma((4,)), dma((4,)), dma((8,)), dma((8,)), dma((8,)), dma((8,)),
             dma((8,)), dma((8,)), dma, dma, dma((8,)), dma((8,)), dma((8,)), dma((8,)),

time: 65.7 us -> 64 us (0.974)
  the two profiles are of different devices: /device:TPU:22 before, /device:TPU:0 now
where the time goes in v7:
time: 64 us; the launch traced here: 63.8 us
  Pallas kernels  59.5 us (93%)
  local copies, waits for them, and re-layouts  3.6 us (6%)
  between operations  0.65 us (1%)
    pallas_call x1, Pallas kernels, per_device(): pl.pallas_call(kernel, name='lightning', out_shape=tuple((pltpu.VMEM(x.sh...  59.5 us
    unnamed x3, local copies, waits for them, and re-layouts  3.6 us

profile of v7, /device:TPU:0, one launch (start us, length us, event | category | flops | bytes accessed | tf_op | source)
XLA Modules:
  0.0 63.8 jit_solution(15574078064217989626)
XLA Ops:
  0.6 59.5 %lightning.1 = (bf16[512,32,128]{2,1,0:T(8,128)(2,1)S(1)}, f32[64,2,16,128]{3,2,1,0:T(8,128)S(1)}, f32[2,6144]{1,0:T(2,128)S(1)}) custom-call(s32[8]{0:T(128)} %slot_ref.1, bf16[512,32,128]{2,1,0:T(8,128)(2,1)} %bitcast.18, bf16[512,32,128]{2,1,0:T(8,128)(2,1)} %bitcast.19, bf16[512,32,128]{2,1,0:T(8,128)(2,1)} %bitcast.20, f32[32,512]{1,0:T(8,128)} %bitcast.24, ...), custom_call_target="tpu_custom_call" | custom-call | tf_op jit(solution)/shard_map/lightning/pallas_call | solution.py:695
  60.2 2.0 %copy.20 = bf16[1,512,32,128]{3,2,1,0:T(8,128)(2,1)} copy(bf16[1,512,32,128]{3,2,1,0:T(8,128)(2,1)S(1)} %bitcast.16) | data formatting | bytes 8388608
  62.2 1.0 %copy.21 = f32[64,2,128,16]{2,3,1,0:T(8,128)} copy(f32[64,2,128,16]{2,3,1,0:T(8,128)S(1)} %bitcast.17) | data formatting | bytes 2097152
  63.2 0.6 copy.22

commit v8 on v7

--- a/solution.py
+++ b/solution.py
@@ -393,6 +393,31 @@
         def _():
             pcur[r] = through(row_total[own_row, r], through(twin_total[own_row, r], start_ref[r]))
 
+    def before_chip(j, _):
+        row = lax.div(j, 4)
+        pbuf[j] = row_start[row]
+
+        @pl.when(lax.rem(j, 4) != x)
+        def _():
+            copy_2(j).start()
+
+        for r in range(2):
+            row_start[row, r] = through(rbuf[j, r], row_start[row, r])
+        return 0
+
+    remote(start_ref, start_all.at[rows[0]], ss, rs, twin).wait_recv()
+
+    @pl.when(own_row == 0)
+    def _():
+        row_start[...] = start_all[...]
+        lax.fori_loop(0, 8, before_chip, 0)
+
+    @pl.when(own_row == 1)
+    def _():
+        for r in range(2):
+            row_start[1, r] = through(twin_total[1, r], start_all[1, r])
+        lax.fori_loop(4, 8, before_chip, 0)
+
     def wait_v(d, _):
         arrival_v(lax.rem(g + d, 8)).wait_recv()
         return 0
@@ -428,32 +453,13 @@
 
     lax.fori_loop(1, 8, send_y, 0)
 
-    remote(start_ref, start_all.at[rows[0]], ss, rs, twin).wait_recv()
-
-    @pl.when(own_row == 0)
-    def _():
-        row_start[...] = start_all[...]
-
     @pl.when(own_row == 1)
     def _():
         copy_t(0).wait_recv()
-        for row in range(2):
-            for r in range(2):
-                row_start[row, r] = through(twin_total[row, r], start_all[row, r])
-
-    def before_chip(j, _):
-        row = lax.div(j, 4)
-        pbuf[j] = row_start[row]
-
-        @pl.when(lax.rem(j, 4) != x)
-        def _():
-            copy_2(j).start()
-
         for r in range(2):
-            row_start[row, r] = through(rbuf[j, r], row_start[row, r])
-        return 0
-
-    lax.fori_loop(0, 8, before_chip, 0)
+            row_start[0, r] = through(twin_total[0, r], start_all[0, r])
+        lax.fori_loop(0, 4, before_chip, 0)
+
     for row in range(2):
         qbuf[4 * row + x] = pbuf[4 * row + x]
     ybuf[g] = ymine[...]

time: 64 us -> 60.3 us (0.942)
  Pallas kernels: 59.5 us -> 55.9 us
    pallas_call x1, Pallas kernels: 59.5 us -> 55.9 us  [per_device(): pl.pallas_call(kernel, name='lightning', out_shape=tuple((pltpu.VMEM(x.sh...]
where the time goes in v8:
time: 60.3 us; the launch traced here: 60.1 us
  Pallas kernels  55.9 us (93%)
  local copies, waits for them, and re-layouts  3.6 us (6%)
  between operations  0.65 us (1%)
    pallas_call x1, Pallas kernels, per_device(): pl.pallas_call(kernel, name='lightning', out_shape=tuple((pltpu.VMEM(x.sh...  55.9 us
    unnamed x3, local copies, waits for them, and re-layouts  3.6 us

profile of v8, /device:TPU:0, one launch (start us, length us, event | category | flops | bytes accessed | tf_op | source)
XLA Modules:
  0.0 60.1 jit_solution(15499368818329599236)
XLA Ops:
  0.6 55.9 %lightning.1 = (bf16[512,32,128]{2,1,0:T(8,128)(2,1)S(1)}, f32[64,2,16,128]{3,2,1,0:T(8,128)S(1)}, f32[2,6144]{1,0:T(2,128)S(1)}) custom-call(s32[8]{0:T(128)} %slot_ref.1, bf16[512,32,128]{2,1,0:T(8,128)(2,1)} %bitcast.18, bf16[512,32,128]{2,1,0:T(8,128)(2,1)} %bitcast.19, bf16[512,32,128]{2,1,0:T(8,128)(2,1)} %bitcast.20, f32[32,512]{1,0:T(8,128)} %bitcast.24, ...), custom_call_target="tpu_custom_call" | custom-call | tf_op jit(solution)/shard_map/lightning/pallas_call | solution.py:701
  56.5 2.0 %copy.20 = bf16[1,512,32,128]{3,2,1,0:T(8,128)(2,1)} copy(bf16[1,512,32,128]{3,2,1,0:T(8,128)(2,1)S(1)} %bitcast.16) | data formatting | bytes 8388608
  58.5 1.0 %copy.21 = f32[64,2,128,16]{2,3,1,0:T(8,128)} copy(f32[64,2,128,16]{2,3,1,0:T(8,128)S(1)} %bitcast.17) | data formatting | bytes 2097152
  59.5 0.6 %copy.22 = f32[2,6144]{1,0:T(2,128)} copy(f32[2,6144]{1,0:T(2,128)S(1)} %get-tuple-element.11) | data formatting | bytes 98304
